TPU v7x, 128 devices: a whole 4x4x4 slice. The times are simulated.
128 devices in a mesh: row: 8 (over z_lo, x), col: 16 (over y, z_hi, core).
Axes of the slice: x: 4, y: 4, z: 4 (z_hi: 2, z_lo: 2; z = z_hi * 2 + z_lo), core: 2. Of those that a mesh axis runs over, the one named last changes fastest.
Arguments:
- small_weight: bfloat16 [4096, 4096], P(('row', 'col')), may hold values from -0.09375 to 0.09375
- expand_out: bfloat16 [8192, 4096], P(('row', 'col')), may hold values from -0.09375 to 0.09375
- expand_in: bfloat16 [8192, 4096], P('col'), may hold values from -0.09375 to 0.09375
- activations: bfloat16 [4096, 8192], P('row', 'col'), may hold values from -6 to 6
- cotangent: bfloat16 [4096, 8192], P('row', 'col'), may hold values from -0.125 to 0.125
Outputs:
- grown_out: bfloat16 [4096, 8192], P('row', 'col')
- grown_grad: bfloat16 [8192, 8192], P('row', 'col')
All inputs are finite; a program needn't handle non-finite values.
Results may differ from a plain program's by a relative error of at most 0.019.
Values may be sent and summed in bfloat16 or wider, within the bound.
A program may use at most 128 MiB of HBM per device.

v0:
```python
import jax
import jax.numpy as jnp
from jax import lax
from jax.sharding import PartitionSpec as P


def per_device(small_weight, expand_out, expand_in, activations, cotangent):
    operator_tile = lax.dot_general(
        lax.all_gather(small_weight, "col", axis=0, tiled=True),
        expand_in,
        (((1,), (1,)), ((), ())),
        preferred_element_type=jnp.float32,
    ).astype(jnp.bfloat16)
    operator_full = lax.all_gather(operator_tile, "row", axis=0, tiled=True)
    grown_tile = jnp.dot(
        lax.all_gather(expand_out, "col", axis=0, tiled=True),
        operator_full,
        preferred_element_type=jnp.float32,
    ).astype(jnp.bfloat16)
    partial_out = lax.dot_general(
        activations,
        lax.all_gather(grown_tile, "row", axis=0, tiled=True),
        (((1,), (1,)), ((), ())),
        preferred_element_type=jnp.float32,
    )
    grown_out = lax.psum_scatter(
        partial_out.astype(jnp.bfloat16), "col", scatter_dimension=1, tiled=True
    )
    cotangent_full = lax.all_gather(cotangent, "col", axis=1, tiled=True)
    summed = lax.psum_scatter(
        lax.dot_general(
            cotangent_full,
            activations,
            (((0,), (0,)), ((), ())),
            preferred_element_type=jnp.float32,
        ).astype(jnp.bfloat16),
        "row",
        scatter_dimension=0,
        tiled=True,
    )
    return (grown_out, summed)


def solution(mesh):
    in_specs = (
        P(("row", "col"), None),
        P(("row", "col"), None),
        P("col", None),
        P("row", "col"),
        P("row", "col"),
    )
    out_specs = (P("row", "col"), P("row", "col"))
    return jax.shard_map(
        per_device, mesh=mesh, in_specs=in_specs, out_specs=out_specs, check_vma=False
    )
```

profile of v0, /device:TPU:1, one launch (start us, length us, event | category | flops | bytes accessed | tf_op | source)
XLA Modules:
  0.0 589.2 jit_solution(18128179400242554788)
XLA Ops:
  7.2 0.0 all-gather.6.cloned.1.call-start
  7.2 0.7 all-gather.6.cloned.1.call-update
  7.9 0.0 all-gather.8.cloned.1.call-start
  8.0 62.2 %all-gather.6.cloned.1.call-done = bf16[512,4096]{1,0:T(8,128)(2,1)} async-done(((bf16[32,4096]{1,0:T(8,128)(2,1)}), bf16[512,4096]{1,0:T(8,128)(2,1)}) %all-gather.6.cloned.1.call-update) | async-done | bytes 4194320 | tf_op jit(solution)/shard_map/all_gather | solution.py:9
  70.2 6.6 %convolution_convert_fusion.3 = bf16[512,512]{1,0:T(8,128)(2,1)} fusion(bf16[512,4096]{1,0:T(8,128)(2,1)} %all-gather.6.cloned.1.call-done, bf16[512,4096]{1,0:T(8,128)(2,1)} %param.7), kind=kOutput, calls=%fused_computation.5 | convolution fusion | flops 2147745792 | bytes 8912896 | tf_op jit(solution)/shard_map/dot_general | solution.py:8
  76.8 0.0 all-gather.10.cloned.1.call-start
  76.9 0.7 all-gather.10.cloned.1.call-update
  77.6 0.0 all-gather.12.cloned.1.call-start
  77.6 50.2 %all-gather.8.cloned.1.call-done = bf16[4096,512]{1,0:T(8,128)(2,1)} async-done(((bf16[512,512]{1,0:T(8,128)(2,1)}), bf16[4096,512]{1,0:T(8,128)(2,1)}) %all-gather.8.cloned.1.call-update) | async-done | bytes 4194320 | tf_op jit(solution)/shard_map/all_gather | solution.py:14
  127.8 74.4 %all-gather.10.cloned.1.call-done = bf16[1024,4096]{1,0:T(8,128)(2,1)} async-done(((bf16[64,4096]{1,0:T(8,128)(2,1)}), bf16[1024,4096]{1,0:T(8,128)(2,1)}) %all-gather.10.cloned.1.call-update) | async-done | bytes 8388624 | tf_op jit(solution)/shard_map/all_gather | solution.py:16
  202.2 10.2 %fusion.1 = bf16[1024,512]{0,1:T(8,128)(2,1)} fusion(bf16[4096,512]{1,0:T(8,128)(2,1)} %all-gather.8.cloned.1.call-done, bf16[1024,4096]{1,0:T(8,128)(2,1)} %all-gather.10.cloned.1.call-done), kind=kOutput, calls=%fused_computation.4 | convolution fusion | flops 4295491584 | bytes 13631488 | tf_op jit(solution)/shard_map/dot_general | solution.py:15
  212.4 0.0 all-gather.12.cloned.1.call-update
  212.4 0.0 all-gather.14.cloned.1.call-start
  212.4 0.5 all-gather.14.cloned.1.call-update
  213.0 0.0 reduce-scatter.3.cloned.1.call-start
  213.0 88.6 %all-gather.12.cloned.1.call-done = bf16[8192,512]{0,1:T(8,128)(2,1)} async-done(((bf16[1024,512]{0,1:T(8,128)(2,1)}), bf16[8192,512]{0,1:T(8,128)(2,1)}) %all-gather.12.cloned.1.call-update) | async-done | bytes 8388624 | tf_op jit(solution)/shard_map/all_gather | solution.py:22
  301.7 10.3 %fusion = bf16[512,8192]{0,1:T(8,128)(2,1)} fusion(bf16[8192,512]{0,1:T(8,128)(2,1)} %all-gather.12.cloned.1.call-done, bf16[512,512]{1,0:T(8,128)(2,1)S(1)} %copy-done), kind=kOutput, calls=%fused_computation.2 | convolution fusion | flops 4299161600 | bytes 17301504 | tf_op jit(solution)/shard_map/dot_general | solution.py:20
  311.9 0.0 reduce-scatter.3.cloned.1.call-update
  311.9 0.2 reduce-scatter.5.cloned.1.call-start
  312.2 71.1 %all-gather.14.cloned.1.call-done = bf16[512,8192]{1,0:T(8,128)(2,1)} async-done(((bf16[512,512]{1,0:T(8,128)(2,1)}), bf16[512,8192]{1,0:T(8,128)(2,1)}) %all-gather.14.cloned.1.call-update) | async-done | bytes 8388624 | tf_op jit(solution)/shard_map/all_gather | solution.py:29
  383.2 10.3 %convolution_convert_fusion = bf16[8192,512]{1,0:T(8,128)(2,1)} fusion(bf16[512,8192]{1,0:T(8,128)(2,1)} %all-gather.14.cloned.1.call-done, bf16[512,512]{1,0:T(8,128)(2,1)S(1)} %copy-done), kind=kOutput, calls=%fused_computation | convolution fusion | flops 4299161600 | bytes 17301504 | tf_op jit(solution)/shard_map/dot_general | solution.py:31
  393.5 93.4 %reduce-scatter.3.cloned.1.call-done = bf16[512,512]{0,1:T(8,128)(2,1)} async-done(((bf16[512,8192]{0,1:T(8,128)(2,1)}), bf16[512,512]{0,1:T(8,128)(2,1)}) %reduce-scatter.3.cloned.1.call-update) | async-done | bytes 524304 | tf_op jit(solution)/shard_map/reduce_scatter | solution.py:26
  486.9 2.0 copy.7
  489.0 93.3 %reduce-scatter.5.cloned.1.call-done = bf16[1024,512]{1,0:T(8,128)(2,1)} async-done(((bf16[8192,512]{1,0:T(8,128)(2,1)}), bf16[1024,512]{1,0:T(8,128)(2,1)}) %reduce-scatter.5.cloned.1.call-update) | async-done | bytes 1048592 | tf_op jit(solution)/shard_map/reduce_scatter | solution.py:30
  (4 shorter events, 0.0 us)
Async XLA Ops:
  7.2 294.5 %copy-start = (bf16[512,512]{1,0:T(8,128)(2,1)S(1)}, bf16[512,512]{1,0:T(8,128)(2,1)}, u32[]{:S(2)}) copy-start(bf16[512,512]{1,0:T(8,128)(2,1)} %param.8) | copy-start | bytes 1572868
  7.2 63.0 %all-gather.6.cloned.1.call-start = ((), (), s32[]{:S(2)}) async-start(), calls=%async_computation.2 | async-start | bytes 4456448 | tf_op jit(solution)/shard_map/all_gather | solution.py:9
  7.9 119.9 %all-gather.8.cloned.1.call-start = ((), (), s32[]{:S(2)}) async-start(), calls=%async_computation.3 | async-start | bytes 4718592 | tf_op jit(solution)/shard_map/all_gather | solution.py:14
  76.8 125.4 %all-gather.10.cloned.1.call-start = ((), (), s32[]{:S(2)}) async-start(), calls=%async_computation.4 | async-start | bytes 8912896 | tf_op jit(solution)/shard_map/all_gather | solution.py:16
  77.6 224.1 %all-gather.12.cloned.1.call-start = ((), (), s32[]{:S(2)}) async-start(), calls=%async_computation.5 | async-start | bytes 9437184 | tf_op jit(solution)/shard_map/all_gather | solution.py:22
  212.4 170.9 %all-gather.14.cloned.1.call-start = ((), (), s32[]{:S(2)}) async-start(), calls=%async_computation.7 | async-start | bytes 8912896 | tf_op jit(solution)/shard_map/all_gather | solution.py:29
  213.0 274.0 %reduce-scatter.3.cloned.1.call-start = ((), (), s32[]{:S(2)}) async-start(), calls=%async_computation.6 | async-start | bytes 8912896 | tf_op jit(solution)/shard_map/reduce_scatter | solution.py:26
  311.9 270.4 %reduce-scatter.5.cloned.1.call-start = ((), (), s32[]{:S(2)}) async-start(), calls=%async_computation.8 | async-start | bytes 9437184 | tf_op jit(solution)/shard_map/reduce_scatter | solution.py:30
Sparse Core Ops, SparseCore 0:
  10.4 59.7 all-gather.5
  76.9 50.8 all-gather.7
  130.2 71.9 all-gather.9
  212.5 89.1 all-gather.11
  303.8 79.4 all-gather.13
  387.4 99.4 reduce-scatter.2
  489.9 92.3 reduce-scatter.4
where the time goes:
time: 589 us
  waiting for transfers between devices  535 us (91%)
  matrix products  37.3 us (6%)
  between operations  14.1 us (2%)
    reduce_scatter x1, waiting for transfers between devices, per_device(): lax.psum_scatter(partial_out.astype(jnp.bfloat16), 'col', scatter_dimensi...  93.4 us
    reduce_scatter x1, waiting for transfers between devices, per_device(): lax.psum_scatter(lax.dot_general(cotangent_full, activations, (((0,), (0,...  93.3 us
    all_gather x1, waiting for transfers between devices, per_device(): lax.all_gather(grown_tile, 'row', axis=0, tiled=True)  88.6 us
    all_gather x1, waiting for transfers between devices, per_device(): lax.all_gather(expand_out, 'col', axis=0, tiled=True)  74.4 us
    all_gather x1, waiting for transfers between devices, per_device(): cotangent_full = lax.all_gather(cotangent, 'col', axis=1, tiled=True)  71.1 us
    all_gather x1, waiting for transfers between devices, per_device(): lax.all_gather(small_weight, 'col', axis=0, tiled=True)  62.2 us
    all_gather x1, waiting for transfers between devices, per_device(): operator_full = lax.all_gather(operator_tile, 'row', axis=0, tiled=True)  50.2 us
  transfers between devices with their start and end apart: 7, of which 7 were waited for; matrix products, arithmetic and copies ran while one was open for 4% of the time, Pallas kernels for 0%

commit v1 on v0

v1 whole, which is shorter than its diff:
```python
import jax
import jax.numpy as jnp
from jax import lax
from jax.experimental import pallas as pl
from jax.experimental.pallas import tpu as pltpu
from jax.sharding import PartitionSpec as P

MESH = pl.DeviceIdType.MESH
F32 = jnp.float32
BF16 = jnp.bfloat16
N_SEM = 96


def dot(a, b, dims):
    return lax.dot_general(a, b, (dims, ((), ())), preferred_element_type=F32)


def kernel(
    sw, eo, ei, act, cot, out_ref, grad_ref,
    s_all, e_all, a_all, c_all, c1_in,
    t_sib, t_sib_in, t_own, t_part, t_tmp, t_two, t_swap, t_swap_in, t_all,
    u_own, u_sib, u_sib_in, u_part, u_in, u_all,
    o_part, o_tmp, o_two, g_part, g_tmp, g_two,
    ssem, rsem,
):
    row, col = lax.axis_index("row"), lax.axis_index("col")
    x, zl = row % 4, row // 4
    k, zh, y = col % 2, (col // 2) % 2, col // 4
    z = zh * 2 + zl
    y0, y1, x0, x1 = y % 2, y // 2, x % 2, x // 2

    def at(x=x, y=y, z=z, k=k):
        return ((z % 2) * 4 + x, (y * 2 + z // 2) * 2 + k)

    def ring(i, d):
        return (i + d) % 4

    def outer(i):
        return ring(i, 3 + 2 * (i % 2))

    sib = at(k=1 - k)
    x_up, x_down = at(x=ring(x, 1)), at(x=ring(x, 3))
    y_up, y_down = at(y=ring(y, 1)), at(y=ring(y, 3))
    z_up, z_down = at(z=ring(z, 1)), at(z=ring(z, 3))
    z_far = at(z=ring(z, 2))

    own_step = 1 - 2 * zh
    c_to = [
        at(x=2 * y0 + zh),
        at(x=2 * y0 + zh, y=ring(y, 4 + own_step)),
        at(x=2 * y0 + 1 - zh),
        at(x=2 * y0 + 1 - zh, y=ring(y, 4 - own_step)),
    ]
    c_slot = [y, ring(y, 4 + own_step), y, ring(y, 4 - own_step)]
    c_self = [x == 2 * y0 + zh, None, x == 2 * y0 + 1 - zh, None]
    c_home = x1 == y0
    c_src_y = jnp.where(c_home, y, ring(y, 4 - (1 - 2 * x0)))
    e_x = jnp.where(zh == 0, x, outer(x))
    e_y = zl * 2 + x1
    e_home = x1 == y0
    e_src_x = jnp.where(e_home, x, outer(x))
    e_src_z = jnp.where(e_home, 0, 2) + y1

    barrier = pltpu.get_barrier_semaphore()

    def greet(to):
        pl.semaphore_signal(barrier, inc=1, device_id=to, device_id_type=MESH)

    expected = 0
    for dz in range(4):
        for dk in range(2):
            if dz or dk:
                greet(at(z=ring(z, dz), k=(k + dk) % 2))
                expected += 1
    for to in (x_up, x_down, y_up, y_down):
        greet(to)
        expected += 1

    def greet_unless_self(to):
        other = jnp.logical_or(to[0] != row, to[1] != col)

        @pl.when(other)
        def _():
            greet(to)

        return other.astype(jnp.int32)

    for to in c_to:
        expected += greet_unless_self(to)
    for i in range(4):
        expected += greet_unless_self(at(x=i, y=c_src_y))
    for i in range(4):
        expected += greet_unless_self(at(x=e_x, y=e_y, z=i, k=y1))
    for i in range(4):
        expected += greet_unless_self(at(x=e_src_x, y=2 * k + i // 2, z=e_src_z, k=i % 2))
    pl.semaphore_wait(barrier, expected)

    count = [0]
    sent = []

    def ids(n):
        first = count[0]
        count[0] += n
        assert count[0] <= N_SEM
        return first

    def remote(src, dst, to, s, r=None):
        return pltpu.make_async_remote_copy(
            src_ref=src, dst_ref=dst, send_sem=ssem.at[s], recv_sem=rsem.at[s if r is None else r],
            device_id=to, device_id_type=MESH,
        )

    def send(src, dst, to, s, r=None):
        copy = remote(src, dst, to, s, r)
        copy.start()
        sent.append((copy, None))

    def send_or_copy(src, dst, to, s, r):
        mine = jnp.logical_and(to[0] == row, to[1] == col)
        copy = remote(src, dst, to, s, r)

        @pl.when(mine)
        def _():
            pltpu.make_async_copy(src, dst, rsem.at[r]).start()

        @pl.when(jnp.logical_not(mine))
        def _():
            copy.start()

        sent.append((copy, jnp.logical_not(mine)))

    def arrived(ref, r):
        remote(ref, ref, sib, r).wait_recv()

    class Gather:
        def __init__(self, slot, first, second, me, up, down):
            self.slot, self.first, self.second, self.me = slot, first, second, me
            self.up, self.down, self.s = up, down, ids(4)

        def start(self):
            mine = self.slot(self.me)
            send(mine, mine, self.up, self.s)
            send(mine, mine, self.down, self.s + 1)

        def pass_up(self):
            i = ring(self.me, 3)
            arrived(self.slot(i), self.s)
            send(self.first(i), self.first(i), self.up, self.s + 2)

        def pass_down(self):
            i = ring(self.me, 1)
            arrived(self.slot(i), self.s + 1)
            send(self.second(i), self.second(i), self.down, self.s + 3)

        def finish(self):
            i = ring(self.me, 2)
            arrived(self.first(i), self.s + 2)
            arrived(self.second(i), self.s + 3)

    class Scatter:
        def __init__(self, slot, first, second, tmp, two, me, up, down):
            self.slot, self.first, self.second = slot, first, second
            self.tmp, self.two, self.me, self.up, self.down, self.s = tmp, two, me, up, down, ids(4)

        def start(self):
            i = ring(self.me, 2)
            send(self.first(i), self.tmp.at[0], self.up, self.s)
            send(self.second(i), self.tmp.at[1], self.down, self.s + 1)

        def pass_up(self):
            i = ring(self.me, 1)
            arrived(self.tmp.at[0], self.s)
            add_into(self.first(i), self.tmp.at[0])
            send(self.slot(i), self.two.at[0], self.up, self.s + 2)

        def pass_down(self):
            i = ring(self.me, 3)
            arrived(self.tmp.at[1], self.s + 1)
            add_into(self.second(i), self.tmp.at[1])
            send(self.slot(i), self.two.at[1], self.down, self.s + 3)

        def finish(self):
            arrived(self.two.at[0], self.s + 2)
            arrived(self.two.at[1], self.s + 3)

    def add_into(dst, src):
        rows = dst.shape[0]

        @pl.loop(0, rows // 64)
        def _(i):
            part = pl.ds(pl.multiple_of(i * 64, 64), 64)
            dst[part] = (dst[part].astype(F32) + src[part].astype(F32)).astype(BF16)

    c1 = ids(1)
    send(cot.at[1 - zh], c1_in, z_far, c1)
    c2s, c2r = ids(4), ids(4)
    for half in range(2):
        send_or_copy(cot.at[zh, half], c_all.at[k, c_slot[half], x], c_to[half], c2s + half, c2r + x)
    a1 = ids(1)
    send(act.at[1 - zh], a_all.at[:, x, :, pl.ds(pl.multiple_of(zh * 512, 512), 512)], z_far, a1)
    s1 = ids(8)
    s_home = s_all.at[zl, x, pl.ds(pl.multiple_of(zh * 64 + k * 32, 32), 32)]
    for dz in (1, 3, 2, 0):
        for dk in range(2):
            tz, tk = ring(z, dz), (k + dk) % 2
            piece = sw.at[:, pl.ds(pl.multiple_of(((tz // 2) * 2 + tk) * 1024, 1024), 1024)]
            if dz or dk:
                send(piece, s_home, at(z=tz, k=tk), s1 + dz * 2 + dk)
            else:
                pltpu.make_async_copy(piece, s_home, rsem.at[s1]).start()
    e1s, e1r = ids(4), ids(4)
    for i in range(4):
        send_or_copy(
            eo.at[:, i * 1024:(i + 1) * 1024], e_all.at[e_x, y0 * 2 + k],
            at(x=e_x, y=e_y, z=i, k=y1), e1s + i, e1r + y0 * 2 + k,
        )
    a_own = ids(1)
    own_cols = a_all.at[:, x, :, pl.ds(pl.multiple_of(zh * 512, 512), 512)]
    pltpu.make_async_copy(act.at[zh], own_cols, rsem.at[a_own]).start()

    acts = act[...].reshape(512, 512)

    def t_block(yy, half, kk):
        cols = pl.ds(pl.multiple_of((half * 2 + kk) * 1024 + yy * 256, 256), 256)
        return dot(acts, ei[:, cols], ((1,), (0,)))

    order = (2, 1, 3, 0)
    t1 = ids(4)
    for d in order:
        for half in range(2):
            t_sib[d, half] = t_block(ring(y, d), half, 1 - k).astype(BF16)
        send(t_sib.at[d], t_sib_in.at[d], sib, t1 + d)
    for d in order:
        for half in range(2):
            t_own[d, half] = t_block(ring(y, d), half, k)

    def t_join(d):
        arrived(t_sib_in.at[d], t1 + d)
        for half in range(2):
            t_part[ring(y, d), half] = (t_own[d, half] + t_sib_in[d, half].astype(F32)).astype(BF16)

    t_sum = Scatter(
        lambda i: t_part.at[i], lambda i: t_part.at[i, 0], lambda i: t_part.at[i, 1], t_tmp, t_two, y, y_up, y_down
    )
    t_join(2)
    t_sum.start()

    arrived(c1_in, c1)
    for half in range(2):
        send_or_copy(
            c1_in.at[half], c_all.at[k, c_slot[2 + half], x], c_to[2 + half], c2s + 2 + half, c2r + x
        )
    t_join(1)
    t_join(3)
    t_sum.pass_up()
    t_sum.pass_down()
    t_join(0)

    for i in range(8):
        arrived(s_home, s1 + i)
    s_ring = Gather(lambda i: s_all.at[:, i], lambda i: s_all.at[0, i], lambda i: s_all.at[1, i], x, x_up, x_down)
    s_ring.start()
    for i in range(4):
        arrived(c_all.at[k, y, i], c2r + i)
    c_ring = Gather(
        lambda i: c_all.at[k, i], lambda i: c_all.at[k, i, 0:2], lambda i: c_all.at[k, i, 2:4], y, y_up, y_down
    )
    c_ring.start()
    c4 = ids(5)
    send(c_all.at[k, y], c_all.at[k, y], sib, c4)
    arrived(own_cols, a_own)
    arrived(a_all.at[:, x, :, pl.ds(pl.multiple_of((1 - zh) * 512, 512), 512)], a1)
    a_ring = Gather(lambda i: a_all.at[:, i], lambda i: a_all.at[0, i], lambda i: a_all.at[1, i], x, x_up, x_down)
    a_ring.start()
    for i in range(4):
        arrived(e_all.at[x, i], e1r + i)
    e_ring = Gather(
        lambda i: e_all.at[i], lambda i: e_all.at[i, 0:2], lambda i: e_all.at[i, 2:4], x, x_up, x_down
    )
    e_ring.start()

    t_sum.finish()
    for half in range(2):
        t_own[0, half] = t_part[y, half].astype(F32) + t_two[0, half].astype(F32) + t_two[1, half].astype(F32)
    t_swap[...] = t_own[0, 1 - zh].astype(BF16)
    t3 = ids(1)
    send(t_swap, t_swap_in, z_far, t3)
    s_ring.pass_up()
    s_ring.pass_down()
    arrived(t_swap_in, t3)
    t_all[y] = (t_own[0, zh] + t_swap_in[...].astype(F32)).astype(BF16)
    t_ring = Gather(
        lambda i: t_all.at[i], lambda i: t_all.at[i, 0:256], lambda i: t_all.at[i, 256:512], y, y_up, y_down
    )
    t_ring.start()
    c_ring.pass_up()
    c_ring.pass_down()
    for n, d in ((1, 3), (2, 1)):
        send(c_all.at[k, ring(y, d)], c_all.at[k, ring(y, d)], sib, c4 + n)
    t_ring.pass_up()
    t_ring.pass_down()
    a_ring.pass_up()
    a_ring.pass_down()
    s_ring.finish()
    t_ring.finish()

    def u_block(n):
        total = None
        for i in range(4):
            part = dot(t_all[i], s_all[n // 4, n % 4, :, i * 256:(i + 1) * 256], ((1,), (1,)))
            total = part if total is None else total + part
        return total

    u1 = ids(1)
    for n in range(8):
        u_own[n % 2, n // 2] = u_block(n)
    u_sib[...] = u_own[1 - k].astype(BF16)
    send(u_sib, u_sib_in, sib, u1)
    e_ring.pass_up()
    e_ring.pass_down()
    arrived(u_sib_in, u1)
    u_part[...] = (u_own[k] + u_sib_in[...].astype(F32)).astype(BF16)
    u2 = ids(4)
    for d in (1, 3, 2):
        send(u_part.at[ring(z, d)], u_in.at[d], at(z=ring(z, d)), u2 + d)
    c_ring.finish()
    for n, half in ((3, slice(0, 2)), (4, slice(2, 4))):
        send(c_all.at[k, ring(y, 2), half], c_all.at[k, ring(y, 2), half], sib, c4 + n)
    for d in (1, 3, 2):
        arrived(u_in.at[d], u2 + d)

    def u_cols(kk, i):
        return pl.ds(pl.multiple_of(kk * 512 + i * 128, 128), 128)

    u_all[zl, :, u_cols(k, y)] = (u_part[z].astype(F32) + u_in[2].astype(F32)).astype(BF16)
    u_all[1 - zl, :, u_cols(k, y)] = (u_in[1].astype(F32) + u_in[3].astype(F32)).astype(BF16)
    u_ring = Gather(
        lambda i: u_all.at[:, :, u_cols(k, i)],
        lambda i: u_all.at[0, :, u_cols(k, i)],
        lambda i: u_all.at[1, :, u_cols(k, i)],
        y, y_up, y_down,
    )
    u_ring.start()
    u4 = ids(5)
    send(u_ring.slot(y), u_ring.slot(y), sib, u4)

    a_ring.finish()
    for n, d in ((0, 0), (1, 3), (2, 1)):
        arrived(c_all.at[1 - k, ring(y, d)], c4 + n)
    for n, half in ((3, slice(0, 2)), (4, slice(2, 4))):
        arrived(c_all.at[1 - k, ring(y, 2), half], c4 + n)

    @pl.loop(0, 8)
    def _(n):
        v, kk, half = n // 4, (n // 2) % 2, n % 2
        home = 2 * v + x1
        away = ring(home, 4 + 1 - 2 * x0)
        cols = pl.ds(pl.multiple_of(half * 512, 512), 512)
        total = dot(
            c_all[kk, home].reshape(512, 512), a_all[0, :, :, cols].reshape(512, 512), ((0,), (0,))
        ) + dot(c_all[kk, away].reshape(512, 512), a_all[1, :, :, cols].reshape(512, 512), ((0,), (0,)))
        g_part[half * 2 + v, pl.ds(pl.multiple_of(kk * 512, 512), 512)] = total.astype(BF16)

    g_sum = Scatter(
        lambda i: g_part.at[i], lambda i: g_part.at[i, 0:512], lambda i: g_part.at[i, 512:1024],
        g_tmp, g_two, z, z_up, z_down,
    )
    g_sum.start()

    u_ring.pass_up()
    u_ring.pass_down()
    for n, d in ((1, 3), (2, 1)):
        send(u_ring.slot(ring(y, d)), u_ring.slot(ring(y, d)), sib, u4 + n)
    e_ring.finish()
    g_sum.pass_up()
    g_sum.pass_down()
    u_ring.finish()
    for n in range(2):
        half = u_all.at[n, :, u_cols(k, ring(y, 2))]
        send(half, half, sib, u4 + 3 + n)
    for n, d in ((0, 0), (1, 3), (2, 1)):
        arrived(u_all.at[:, :, u_cols(1 - k, ring(y, d))], u4 + n)
    for n in range(2):
        arrived(u_all.at[n, :, u_cols(1 - k, ring(y, 2))], u4 + 3 + n)
    for v in range(2):
        for w in range(2):
            slot = 2 * y0 + v
            if w:
                slot = outer(slot)
            weight = e_all[slot].reshape(256, 1024)
            for tok in range(2):
                total = dot(u_all[tok], weight, ((1,), (1,))).astype(BF16)
                for n in range(2):
                    o_part[v * 2 + tok, :, n * 256 + w * 128:n * 256 + w * 128 + 128] = total[:, n * 128:n * 128 + 128]
    o_sum = Scatter(
        lambda i: o_part.at[i], lambda i: o_part.at[i, 0:256], lambda i: o_part.at[i, 256:512],
        o_tmp, o_two, z, z_up, z_down,
    )
    o_sum.start()
    o_sum.pass_up()
    o_sum.pass_down()

    def last(dst, part, two):
        @pl.loop(0, dst.shape[0] // 64)
        def _(i):
            rows = pl.ds(pl.multiple_of(i * 64, 64), 64)
            dst[rows] = (
                part[rows].astype(F32) + two[0, rows].astype(F32) + two[1, rows].astype(F32)
            ).astype(BF16)

    g_sum.finish()
    last(grad_ref, g_part.at[z], g_two)
    o_sum.finish()
    last(out_ref, o_part.at[z], o_two)
    for copy, when in sent:
        if when is None:
            copy.wait_send()
        else:
            pl.when(when)(copy.wait_send)


def per_device(small_weight, expand_out, expand_in, activations, cotangent):
    vmem = pl.BlockSpec(memory_space=pltpu.VMEM)

    def buf(*shape, dtype=BF16):
        return pltpu.VMEM(shape, dtype)

    return pl.pallas_call(
        kernel,
        out_shape=(
            jax.ShapeDtypeStruct((512, 512), BF16),
            jax.ShapeDtypeStruct((1024, 512), BF16),
        ),
        in_specs=[vmem] * 5,
        out_specs=(vmem, vmem),
        scratch_shapes=[
            buf(2, 4, 128, 1024),
            buf(4, 4, 64, 1024),
            buf(2, 4, 128, 1024),
            buf(2, 4, 4, 128, 512),
            buf(2, 128, 512),
            buf(4, 2, 512, 256),
            buf(4, 2, 512, 256),
            buf(4, 2, 512, 256, dtype=F32),
            buf(4, 2, 512, 256),
            buf(2, 512, 256),
            buf(2, 2, 512, 256),
            buf(512, 256),
            buf(512, 256),
            buf(4, 512, 256),
            buf(2, 4, 512, 128, dtype=F32),
            buf(4, 512, 128),
            buf(4, 512, 128),
            buf(4, 512, 128),
            buf(4, 512, 128),
            buf(2, 512, 1024),
            buf(4, 512, 512),
            buf(2, 256, 512),
            buf(2, 512, 512),
            buf(4, 1024, 512),
            buf(2, 512, 512),
            buf(2, 1024, 512),
            pltpu.SemaphoreType.DMA((N_SEM,)),
            pltpu.SemaphoreType.DMA((N_SEM,)),
        ],
        compiler_params=pltpu.CompilerParams(
            collective_id=0, has_side_effects=True, vmem_limit_bytes=58 * 2**20
        ),
        cost_estimate=pl.CostEstimate(flops=9_700_000_000, bytes_accessed=8_000_000, transcendentals=0),
        name="grow",
    )(
        small_weight,
        expand_out,
        expand_in,
        activations.reshape(2, 2, 128, 512),
        cotangent.reshape(2, 2, 128, 512),
    )


def solution(mesh):
    in_specs = (
        P(("row", "col"), None),
        P(("row", "col"), None),
        P("col", None),
        P("row", "col"),
        P("row", "col"),
    )
    out_specs = (P("row", "col"), P("row", "col"))
    return jax.shard_map(per_device, mesh=mesh, in_specs=in_specs, out_specs=out_specs, check_vma=False)
```

time: 589 us -> 175 us (0.30)
  waiting for transfers between devices: 535 us -> 0 us
  Pallas kernels: 0 us -> 170 us
  matrix products: 37.3 us -> 0 us
  between operations: 14.1 us -> 0.64 us
    all_gather x5 -> x0, waiting for transfers between devices: 346 us -> none  [the longest x1 88.6 us: per_device(): lax.all_gather(grown_tile, 'row', axis=0, tiled=True)]
    reduce_scatter x2 -> x0, waiting for transfers between devices: 187 us -> none  [the longest x1 93.4 us: per_device(): lax.psum_scatter(partial_out.astype(jnp.bfloat16), 'col', scatter_dimensi...]
    pallas_call x0 -> x1, Pallas kernels: none -> 170 us  [per_device(): pl.pallas_call(kernel, out_shape=(jax.ShapeDtypeStruct((512, 512), BF16),...]
    dot_general x4 -> x0, matrix products: 37.3 us -> none  [the longest x1 10.3 us: per_device(): lax.dot_general(activations, lax.all_gather(grown_tile, 'row', axis=0, ti...]
  transfers between devices with their start and end apart: 7 -> 0, of which waited for: 7 -> 0; matrix products, arithmetic and copies ran while one was open for 4% -> 0% of each run, Pallas kernels for 0% -> 0%
where the time goes in v1:
time: 175 us; the launch traced here: 174 us
  Pallas kernels  170 us (97%)
  local copies, waits for them, and re-layouts  4.13 us (2%)
    pallas_call x1, Pallas kernels, per_device(): pl.pallas_call(kernel, out_shape=(jax.ShapeDtypeStruct((512, 512), BF16),...  170 us
    unnamed x2, local copies, waits for them, and re-layouts  4.13 us

profile of v1, /device:TPU:1, one launch (start us, length us, event | category | flops | bytes accessed | tf_op | source)
XLA Modules:
  0.0 174.3 jit_solution(6925670502965380277)
XLA Ops:
  0.6 169.5 %grow.1 = (bf16[512,512]{1,0:T(8,128)(2,1)}, bf16[1024,512]{1,0:T(8,128)(2,1)}) custom-call(bf16[32,4096]{1,0:T(8,128)(2,1)} %sw.1, bf16[64,4096]{1,0:T(8,128)(2,1)} %eo.1, bf16[512,4096]{1,0:T(8,128)(2,1)} %ei.1, bf16[2,2,128,512]{3,2,1,0:T(8,128)(2,1)} %bitcast.2, bf16[2,2,128,512]{3,2,1,0:T(8,128)(2,1)} %bitcast.3), custom_call_target="tpu_custom_call" | custom-call | flops 9699999744 | bytes 8000000 | tf_op jit(solution)/shard_map/grow/pallas_call | solution.py:428
  170.2 1.9 %copy.9 = bf16[512,512]{1,0:T(8,128)(2,1)} copy(bf16[512,512]{1,0:T(8,128)(2,1)} %get-tuple-element.4) | data formatting | bytes 1048576
  172.0 2.3 %copy.10 = bf16[1024,512]{1,0:T(8,128)(2,1)} copy(bf16[1024,512]{1,0:T(8,128)(2,1)} %get-tuple-element.5) | data formatting | bytes 2097152

commit v2 on v1

v2 whole, which is shorter than its diff:
```python
import jax
import jax.numpy as jnp
from jax import lax
from jax.experimental import pallas as pl
from jax.experimental.pallas import tpu as pltpu
from jax.sharding import PartitionSpec as P

MESH = pl.DeviceIdType.MESH
F32 = jnp.float32
BF16 = jnp.bfloat16
N_SEM = 160


def dot(a, b, dims):
    return lax.dot_general(a, b, (dims, ((), ())), preferred_element_type=F32)


def kernel(
    sw, eo, ei_hbm, act_hbm, cot, out_ref, grad_ref,
    ei, act, in_sem, s_all, e_z, e_all, out_v, grad_v, out_sem, a_all, c_all, c_spread, c1_in,
    t_sib, t_sib_in, t_own, t_part, t_tmp, t_two, t_swap, t_swap_in, t_all,
    u_own, u_sib, u_sib_in, u_part, u_in, u_all,
    o_part, o_tmp, o_two, g_part, g_tmp, g_two,
    ssem, rsem,
):
    row, col = lax.axis_index("row"), lax.axis_index("col")
    x, zl = row % 4, row // 4
    k, zh, y = col % 2, (col // 2) % 2, col // 4
    z = zh * 2 + zl
    y0, y1, x0, x1 = y % 2, y // 2, x % 2, x // 2

    def at(x=x, y=y, z=z, k=k):
        return ((z % 2) * 4 + x, (y * 2 + z // 2) * 2 + k)

    def ring(i, d):
        return (i + d) % 4

    def outer(i):
        return ring(i, 3 + 2 * (i % 2))

    sib = at(k=1 - k)
    x_up, x_down = at(x=ring(x, 1)), at(x=ring(x, 3))
    y_up, y_down = at(y=ring(y, 1)), at(y=ring(y, 3))
    z_up, z_down = at(z=ring(z, 1)), at(z=ring(z, 3))
    z_far = at(z=ring(z, 2))

    c_x = [[2 * y0 + zh, 2 * (1 - y0) + zh], [2 * y0 + 1 - zh, 2 * (1 - y0) + 1 - zh]]
    c_home = x1 == y0
    e_x = [x, x, outer(x), outer(x)]
    e_to = [at(x=e_x[i], y=(i % 2) * 2 + x1, k=y1) for i in range(4)]
    e_src_x = jnp.where(c_home, x, outer(x))

    order = (2, 1, 3, 0)
    act_copy = pltpu.make_async_copy(act_hbm, act, in_sem.at[16])
    act_copy.start()

    def ei_copies(d):
        return [
            pltpu.make_async_copy(
                ei_hbm.at[:, pl.ds(pl.multiple_of(q * 1024 + ring(y, d) * 256, 256), 256)], ei.at[d, q], in_sem.at[d * 4 + q]
            )
            for q in range(4)
        ]

    def a_cols(half):
        return pl.ds(pl.multiple_of(half * 512, 512), 512)

    a_own_copy = pltpu.make_async_copy(act_hbm.at[zh], a_all.at[:, x, :, a_cols(zh)], in_sem.at[17])
    a_own_copy.start()
    for d in order:
        for copy in ei_copies(d):
            copy.start()

    barrier = pltpu.get_barrier_semaphore()

    def greet(to):
        pl.semaphore_signal(barrier, inc=1, device_id=to, device_id_type=MESH)

    expected = 0
    for dz in range(4):
        for dk in range(2):
            if dz or dk:
                greet(at(z=ring(z, dz), k=(k + dk) % 2))
                expected += 1
    for to in (x_up, x_down, y_up, y_down):
        greet(to)
        expected += 1

    def greet_unless_self(to):
        other = jnp.logical_or(to[0] != row, to[1] != col)

        @pl.when(other)
        def _():
            greet(to)

        return other.astype(jnp.int32)

    for d in (2,):
        greet(at(x=ring(x, d)))
        expected += 1
    for to in e_to:
        expected += greet_unless_self(to)
    for i in range(4):
        expected += greet_unless_self(at(x=e_src_x, y=2 * k + i // 2, k=i % 2))
    count = [0]
    sent = []

    def ids(n):
        first = count[0]
        count[0] += n
        assert count[0] <= N_SEM
        return first

    def remote(src, dst, to, s, r=None):
        return pltpu.make_async_remote_copy(
            src_ref=src, dst_ref=dst, send_sem=ssem.at[s], recv_sem=rsem.at[s if r is None else r],
            device_id=to, device_id_type=MESH,
        )

    def send(src, dst, to, s, r=None):
        copy = remote(src, dst, to, s, r)
        copy.start()
        sent.append((copy, None))

    def send_or_copy(src, dst, to, s, r):
        mine = jnp.logical_and(to[0] == row, to[1] == col)
        copy = remote(src, dst, to, s, r)

        @pl.when(mine)
        def _():
            pltpu.make_async_copy(src, dst, rsem.at[r]).start()

        @pl.when(jnp.logical_not(mine))
        def _():
            copy.start()

        sent.append((copy, jnp.logical_not(mine)))

    def arrived(ref, r):
        remote(ref, ref, sib, r).wait_recv()

    class Gather:
        def __init__(self, slot, first, second, me, up, down):
            self.slot, self.first, self.second, self.me = slot, first, second, me
            self.up, self.down, self.s = up, down, ids(4)

        def start(self):
            mine = self.slot(self.me)
            send(mine, mine, self.up, self.s)
            send(mine, mine, self.down, self.s + 1)

        def pass_up(self):
            i = ring(self.me, 3)
            arrived(self.slot(i), self.s)
            send(self.first(i), self.first(i), self.up, self.s + 2)

        def pass_down(self):
            i = ring(self.me, 1)
            arrived(self.slot(i), self.s + 1)
            send(self.second(i), self.second(i), self.down, self.s + 3)

        def finish(self):
            i = ring(self.me, 2)
            arrived(self.first(i), self.s + 2)
            arrived(self.second(i), self.s + 3)

    class Scatter:
        def __init__(self, slot, first, second, tmp, two, me, up, down):
            self.slot, self.first, self.second = slot, first, second
            self.tmp, self.two, self.me, self.up, self.down, self.s = tmp, two, me, up, down, ids(4)

        def start(self):
            i = ring(self.me, 2)
            send(self.first(i), self.tmp.at[0], self.up, self.s)
            send(self.second(i), self.tmp.at[1], self.down, self.s + 1)

        def pass_up(self):
            i = ring(self.me, 1)
            arrived(self.tmp.at[0], self.s)
            add_into(self.first(i), self.tmp.at[0])
            send(self.slot(i), self.two.at[0], self.up, self.s + 2)

        def pass_down(self):
            i = ring(self.me, 3)
            arrived(self.tmp.at[1], self.s + 1)
            add_into(self.second(i), self.tmp.at[1])
            send(self.slot(i), self.two.at[1], self.down, self.s + 3)

        def finish(self):
            arrived(self.two.at[0], self.s + 2)
            arrived(self.two.at[1], self.s + 3)

    def add_into(dst, src):
        rows = dst.shape[0]

        @pl.loop(0, rows // 64)
        def _(i):
            part = pl.ds(pl.multiple_of(i * 64, 64), 64)
            dst[part] = (dst[part].astype(F32) + src[part].astype(F32)).astype(BF16)

    sp, c1, a1, s1, e1, e2s, e2r = ids(2), ids(2), ids(1), ids(8), ids(4), ids(4), ids(4)
    c2s, c2r = [ids(4), ids(4)], [ids(4), ids(4)]
    t1, t3, u1 = ids(4), ids(2), ids(2)
    u2, u4 = [ids(4), ids(4)], [ids(5), ids(5)]
    c4 = [ids(5), ids(5)]
    s_home = s_all.at[zl, x, pl.ds(pl.multiple_of(zh * 64 + k * 32, 32), 32)]

    def spread_send():
        for n, to in enumerate((y_up, y_down)):
            send(cot.at[:, 1, n * 64:n * 64 + 64], c_spread.at[:, n * 64:n * 64 + 64], to, sp + n)

    def c1_send(half):
        src = cot.at[1 - zh, 0] if half == 0 else c_spread.at[1 - zh]
        send(src, c1_in.at[half], z_far, c1 + half)

    def a1_send():
        send(act_hbm.at[1 - zh], a_all.at[:, x, :, a_cols(zh)], z_far, a1)

    def c2_send(other, half):
        if other:
            src = c1_in.at[half]
        else:
            src = c_spread.at[zh] if half else cot.at[zh, 0]
        for j in range(2):
            send_or_copy(
                src.at[:, j * 256:(j + 1) * 256], c_all.at[k, j, y, x], at(x=c_x[other][half]),
                c2s[j] + 2 * other + half, c2r[j] + x,
            )

    def s1_send():
        for dz in (1, 3, 2, 0):
            for dk in range(2):
                tz, tk = ring(z, dz), (k + dk) % 2
                piece = sw.at[:, pl.ds(pl.multiple_of(((tz // 2) * 2 + tk) * 1024, 1024), 1024)]
                if dz or dk:
                    send(piece, s_home, at(z=tz, k=tk), s1 + dz * 2 + dk)
                else:
                    pltpu.make_async_copy(piece, s_home, rsem.at[s1]).start()

    def e1_send():
        for d in (1, 3, 2, 0):
            i = ring(z, d)
            piece = eo.at[:, pl.ds(pl.multiple_of(i * 1024, 1024), 1024)]
            if d:
                send(piece, e_z.at[z], at(z=i), e1 + d)
            else:
                pltpu.make_async_copy(piece, e_z.at[z], rsem.at[e1]).start()

    def e2_send():
        for d in range(4):
            arrived(e_z.at[ring(z, 4 - d)], e1 + d)
        for i in range(4):
            send_or_copy(e_z.at[i], e_all.at[e_x[i], y0 * 2 + k], e_to[i], e2s + i, e2r + y0 * 2 + k)

    def e_enter():
        for i in range(4):
            arrived(e_all.at[x, i], e2r + i)
        e_ring.start()

    s_ring = Gather(lambda i: s_all.at[:, i], lambda i: s_all.at[0, i], lambda i: s_all.at[1, i], x, x_up, x_down)
    a_ring = [
        Gather(
            lambda i, c=c: a_all.at[:, i, :, c], lambda i, c=c: a_all.at[0, i, :, c],
            lambda i, c=c: a_all.at[1, i, :, c], x, x_up, x_down,
        )
        for c in (a_cols(zh), a_cols(1 - zh))
    ]
    e_ring = Gather(
        lambda i: e_all.at[i], lambda i: e_all.at[i, 0:2], lambda i: e_all.at[i, 2:4], x, x_up, x_down
    )
    c_ring = [
        Gather(
            lambda i, j=j: c_all.at[k, j, i], lambda i, j=j: c_all.at[k, j, i, 0:2],
            lambda i, j=j: c_all.at[k, j, i, 2:4], y, y_up, y_down,
        )
        for j in range(2)
    ]
    t_ring = [
        Gather(
            lambda i, c=c: t_all.at[i, c * 256:c * 256 + 256], lambda i, c=c: t_all.at[i, c * 256:c * 256 + 128],
            lambda i, c=c: t_all.at[i, c * 256 + 128:c * 256 + 256], y, y_up, y_down,
        )
        for c in range(2)
    ]

    def u_cols(kk, i):
        return pl.ds(pl.multiple_of(kk * 512 + i * 128, 128), 128)

    def u_block(c, kk, i, tok=slice(None)):
        return u_all.at[tok, c * 256:c * 256 + 256, u_cols(kk, i)]

    u_ring = [
        Gather(
            lambda i, c=c: u_block(c, k, i), lambda i, c=c: u_block(c, k, i, 0), lambda i, c=c: u_block(c, k, i, 1),
            y, y_up, y_down,
        )
        for c in range(2)
    ]
    t_sum = Scatter(
        lambda i: t_part.at[i], lambda i: t_part.at[i, 0], lambda i: t_part.at[i, 1], t_tmp, t_two, y, y_up, y_down
    )
    g_sum = [
        Scatter(
            lambda i, j=j: g_part.at[j, i], lambda i, j=j: g_part.at[j, i, 0:256],
            lambda i, j=j: g_part.at[j, i, 256:512], g_tmp.at[j], g_two.at[j], z, z_up, z_down,
        )
        for j in range(2)
    ]
    o_sum = [
        Scatter(
            lambda i, c=c: o_part.at[c, i], lambda i, c=c: o_part.at[c, i, 0:128],
            lambda i, c=c: o_part.at[c, i, 128:256], o_tmp.at[c], o_two.at[c], z, z_up, z_down,
        )
        for c in range(2)
    ]

    def t_dots(d, kk, dst):
        for half in range(2):
            dst[d, half] = dot(act[...].reshape(512, 512), ei[d, half * 2 + kk], ((1,), (0,))).astype(dst.dtype)

    def t_join(d):
        arrived(t_sib_in.at[d], t1 + d)
        for half in range(2):
            t_part[ring(y, d), half] = (t_own[d, half] + t_sib_in[d, half].astype(F32)).astype(BF16)

    act_copy.wait()
    for d in order:
        for copy in ei_copies(d):
            copy.wait()
    t_dots(2, 1 - k, t_sib)
    a_own_copy.wait()
    pl.semaphore_wait(barrier, expected)
    send(t_sib.at[2], t_sib_in.at[2], sib, t1 + 2)
    spread_send()
    c1_send(0)
    c2_send(0, 0)
    a_ring[0].start()
    a1_send()
    t_dots(2, k, t_own)
    for d in order[1:]:
        t_dots(d, 1 - k, t_sib)
        send(t_sib.at[d], t_sib_in.at[d], sib, t1 + d)
    t_join(2)
    t_sum.start()
    for d in order[1:]:
        t_dots(d, k, t_own)
    for d in order[1:]:
        t_join(d)
    for n in range(2):
        arrived(c_spread.at[:, n * 64:n * 64 + 64], sp + n)
    c1_send(1)
    c2_send(0, 1)
    arrived(c1_in.at[0], c1)
    c2_send(1, 0)
    s1_send()
    t_sum.pass_up()
    t_sum.pass_down()

    def c_enter(j):
        for i in range(4):
            arrived(c_all.at[k, j, y, i], c2r[j] + i)
        c_ring[j].start()
        send(c_all.at[k, j, y], c_all.at[k, j, y], sib, c4[j])

    def c_pass(j):
        c_ring[j].pass_up()
        c_ring[j].pass_down()
        for n, d in ((1, 3), (2, 1)):
            send(c_all.at[k, j, ring(y, d)], c_all.at[k, j, ring(y, d)], sib, c4[j] + n)

    def c_finish(j):
        c_ring[j].finish()
        for n, half in ((3, slice(0, 2)), (4, slice(2, 4))):
            send(c_all.at[k, j, ring(y, 2), half], c_all.at[k, j, ring(y, 2), half], sib, c4[j] + n)

    def c_sibling(j):
        for n, d in ((0, 0), (1, 3), (2, 1)):
            arrived(c_all.at[1 - k, j, ring(y, d)], c4[j] + n)
        for n, half in ((3, slice(0, 2)), (4, slice(2, 4))):
            arrived(c_all.at[1 - k, j, ring(y, 2), half], c4[j] + n)

    arrived(a_all.at[:, x, :, a_cols(1 - zh)], a1)
    a_ring[1].start()
    arrived(c1_in.at[1], c1 + 1)
    c2_send(1, 1)
    a_ring[0].pass_up()
    a_ring[0].pass_down()
    c_enter(0)

    def t_enter(c):
        rows = slice(c * 256, c * 256 + 256)
        arrived(t_swap_in.at[rows], t3 + c)
        t_all[y, rows] = (t_own[0, zh, rows] + t_swap_in[rows].astype(F32)).astype(BF16)
        t_ring[c].start()

    t_sum.finish()
    for c in range(2):
        rows = slice(c * 256, c * 256 + 256)
        for half in range(2):
            t_own[0, half, rows] = (
                t_part[y, half, rows].astype(F32)
                + t_two[0, half, rows].astype(F32)
                + t_two[1, half, rows].astype(F32)
            )
        t_swap[rows] = t_own[0, 1 - zh, rows].astype(BF16)
        send(t_swap.at[rows], t_swap_in.at[rows], z_far, t3 + c)
    e1_send()
    a_ring[1].pass_up()
    a_ring[1].pass_down()
    for i in range(8):
        arrived(s_home, s1 + i)
    s_ring.start()
    c_pass(0)
    c_enter(1)
    t_enter(0)
    t_enter(1)
    c_finish(0)
    for ring_of_a in a_ring:
        ring_of_a.finish()
    c_sibling(0)

    def g_block(j):
        @pl.loop(0, 4)
        def _(n):
            v, kk = n // 2, n % 2
            home = 2 * v + x1
            for half in range(2):
                cols = slice(half * 512, half * 512 + 512)
                total = dot(
                    c_all[kk, j, home].reshape(512, 256), a_all[0, :, :, cols].reshape(512, 512), ((0,), (0,))
                )
                for d, toks in ((1, slice(0, 64)), (3, slice(64, 128))):
                    total += dot(
                        c_all[kk, j, ring(home, d), :, toks].reshape(256, 256),
                        a_all[1, :, toks, cols].reshape(256, 512), ((0,), (0,)),
                    )
                g_part[j, half * 2 + v, pl.ds(pl.multiple_of(kk * 256, 256), 256)] = total.astype(BF16)

    g_block(0)
    g_sum[0].start()
    t_ring[0].pass_up()
    t_ring[0].pass_down()
    c_pass(1)
    t_ring[1].pass_up()
    t_ring[1].pass_down()
    s_ring.pass_up()
    s_ring.pass_down()
    g_sum[0].pass_up()
    g_sum[0].pass_down()
    e2_send()
    c_finish(1)
    c_sibling(1)
    g_block(1)
    g_sum[1].start()

    def u_dot(c, n):
        total = None
        for i in range(4):
            part = dot(
                t_all[i, c * 256:c * 256 + 256], s_all[n // 4, n % 4, :, i * 256:(i + 1) * 256], ((1,), (1,))
            )
            total = part if total is None else total + part
        return total

    for c in range(2):
        t_ring[c].finish()
        if c == 0:
            s_ring.finish()
        for n in range(8):
            u_own[c, n % 2, n // 2] = u_dot(c, n)
        u_sib[c] = u_own[c, 1 - k].astype(BF16)
        send(u_sib.at[c], u_sib_in.at[c], sib, u1 + c)
    for c in range(2):
        arrived(u_sib_in.at[c], u1 + c)
        u_part[c] = (u_own[c, k] + u_sib_in[c].astype(F32)).astype(BF16)
        for d in (1, 3, 2):
            send(u_part.at[c, ring(z, d)], u_in.at[c, d], at(z=ring(z, d)), u2[c] + d)
    e_enter()

    def u_enter(c):
        rows = slice(c * 256, c * 256 + 256)
        for d in (1, 3, 2):
            arrived(u_in.at[c, d], u2[c] + d)
        u_all[zl, rows, u_cols(k, y)] = (u_part[c, z].astype(F32) + u_in[c, 2].astype(F32)).astype(BF16)
        u_all[1 - zl, rows, u_cols(k, y)] = (u_in[c, 1].astype(F32) + u_in[c, 3].astype(F32)).astype(BF16)
        u_ring[c].start()
        send(u_block(c, k, y), u_block(c, k, y), sib, u4[c])

    def u_pass(c):
        u_ring[c].pass_up()
        u_ring[c].pass_down()
        for n, d in ((1, 3), (2, 1)):
            send(u_block(c, k, ring(y, d)), u_block(c, k, ring(y, d)), sib, u4[c] + n)

    def u_finish(c):
        u_ring[c].finish()
        for n in range(2):
            half = u_block(c, k, ring(y, 2), n)
            send(half, half, sib, u4[c] + 3 + n)
        for n, d in ((0, 0), (1, 3), (2, 1)):
            arrived(u_block(c, 1 - k, ring(y, d)), u4[c] + n)
        for n in range(2):
            arrived(u_block(c, 1 - k, ring(y, 2), n), u4[c] + 3 + n)

    u_enter(0)
    u_enter(1)
    g_sum[1].pass_up()
    g_sum[1].pass_down()
    e_ring.pass_up()
    e_ring.pass_down()
    u_pass(0)
    u_pass(1)
    u_finish(0)
    e_ring.finish()

    def o_block(c):
        for v in range(2):
            for w in range(2):
                slot = 2 * y0 + v
                if w:
                    slot = outer(slot)
                weight = e_all[slot].reshape(256, 1024)
                for tok in range(2):
                    total = dot(u_all[tok, c * 256:c * 256 + 256], weight, ((1,), (1,))).astype(BF16)
                    for n in range(2):
                        o_part[c, v * 2 + tok, :, n * 256 + w * 128:n * 256 + w * 128 + 128] = total[
                            :, n * 128:n * 128 + 128
                        ]

    o_block(0)
    o_sum[0].start()
    u_finish(1)
    o_block(1)
    o_sum[1].start()
    g_sum[0].finish()
    o_sum[0].pass_up()
    o_sum[0].pass_down()
    o_sum[1].pass_up()
    o_sum[1].pass_down()

    def last(dst, part, two, first, to):
        @pl.loop(0, 4)
        def _(i):
            src = pl.ds(pl.multiple_of(first + i * 64, 64), 64)
            dst[pl.ds(pl.multiple_of(to + i * 64, 64), 64)] = (
                part[src].astype(F32) + two[0, src].astype(F32) + two[1, src].astype(F32)
            ).astype(BF16)

    g_sum[1].finish()
    for j in range(2):
        for kk in range(2):
            last(grad_v, g_part.at[j, z], g_two.at[j], kk * 256, kk * 512 + j * 256)
    writes = [pltpu.make_async_copy(grad_v, grad_ref, out_sem.at[0])]
    writes[0].start()
    for c in range(2):
        o_sum[c].finish()
        rows = slice(c * 256, c * 256 + 256)
        last(out_v, o_part.at[c, z], o_two.at[c], 0, c * 256)
        writes.append(pltpu.make_async_copy(out_v.at[rows], out_ref.at[rows], out_sem.at[1 + c]))
        writes[-1].start()
    for copy, when in sent:
        if when is None:
            copy.wait_send()
        else:
            pl.when(when)(copy.wait_send)
    for copy in writes:
        copy.wait()


def place(out_in, grad_in, out_ref, grad_ref, rows, in_sem, out_sem):
    parts = [(out_in, out_ref, i) for i in range(2)] + [(grad_in, grad_ref, i) for i in range(4)]
    reads, writes = [], []
    for n, (src, dst, i) in enumerate(parts):
        part = pl.ds(i * 256, 256)
        reads.append(pltpu.make_async_copy(src.at[part], rows.at[n], in_sem.at[n]))
        writes.append(pltpu.make_async_copy(rows.at[n], dst.at[part], out_sem.at[n]))
        reads[n].start()
    for read, write in zip(reads, writes):
        read.wait()
        write.start()
    for write in writes:
        write.wait()


def per_device(small_weight, expand_out, expand_in, activations, cotangent):
    hbm = pl.BlockSpec(memory_space=pl.ANY)

    def buf(*shape, dtype=BF16):
        return pltpu.VMEM(shape, dtype)

    out, grad = pl.pallas_call(
        kernel,
        out_shape=(
            jax.ShapeDtypeStruct((512, 512), BF16),
            jax.ShapeDtypeStruct((1024, 512), BF16),
        ),
        in_specs=[hbm] * 5,
        out_specs=(hbm, hbm),
        scratch_shapes=[
            buf(4, 4, 512, 256),
            buf(2, 2, 128, 512),
            pltpu.SemaphoreType.DMA((18,)),
            buf(2, 4, 128, 1024),
            buf(4, 64, 1024),
            buf(4, 4, 64, 1024),
            buf(512, 512),
            buf(1024, 512),
            pltpu.SemaphoreType.DMA((3,)),
            buf(2, 4, 128, 1024),
            buf(2, 2, 4, 4, 128, 256),
            buf(2, 128, 512),
            buf(2, 128, 512),
            buf(4, 2, 512, 256),
            buf(4, 2, 512, 256),
            buf(4, 2, 512, 256, dtype=F32),
            buf(4, 2, 512, 256),
            buf(2, 512, 256),
            buf(2, 2, 512, 256),
            buf(512, 256),
            buf(512, 256),
            buf(4, 512, 256),
            buf(2, 2, 4, 256, 128, dtype=F32),
            buf(2, 4, 256, 128),
            buf(2, 4, 256, 128),
            buf(2, 4, 256, 128),
            buf(2, 4, 256, 128),
            buf(2, 512, 1024),
            buf(2, 4, 256, 512),
            buf(2, 2, 128, 512),
            buf(2, 2, 256, 512),
            buf(2, 4, 512, 512),
            buf(2, 2, 256, 512),
            buf(2, 2, 512, 512),
            pltpu.SemaphoreType.DMA((N_SEM,)),
            pltpu.SemaphoreType.DMA((N_SEM,)),
        ],
        compiler_params=pltpu.CompilerParams(
            collective_id=0, has_side_effects=True, vmem_limit_bytes=58 * 2**20
        ),
        cost_estimate=pl.CostEstimate(flops=9_700_000_000, bytes_accessed=8_000_000, transcendentals=0),
        name="grow",
    )(
        small_weight,
        expand_out,
        expand_in,
        activations.reshape(2, 2, 128, 512),
        cotangent.reshape(2, 2, 128, 512),
    )
    return pl.pallas_call(
        place,
        out_shape=(jax.ShapeDtypeStruct(out.shape, BF16), jax.ShapeDtypeStruct(grad.shape, BF16)),
        in_specs=[hbm] * 2,
        out_specs=(hbm, hbm),
        scratch_shapes=[buf(6, 256, 512), pltpu.SemaphoreType.DMA((6,)), pltpu.SemaphoreType.DMA((6,))],
        name="place",
    )(out, grad)


def solution(mesh):
    in_specs = (
        P(("row", "col"), None),
        P(("row", "col"), None),
        P("col", None),
        P("row", "col"),
        P("row", "col"),
    )
    out_specs = (P("row", "col"), P("row", "col"))
    return jax.shard_map(per_device, mesh=mesh, in_specs=in_specs, out_specs=out_specs, check_vma=False)
```

time: 175 us -> 118 us (0.67)
  Pallas kernels: 170 us -> 117 us
  local copies, waits for them, and re-layouts: 4.13 us -> 0 us
    pallas_call x1, Pallas kernels: 170 us -> 115 us  [per_device(): pl.pallas_call(kernel, out_shape=(jax.ShapeDtypeStruct((512, 512), BF16),...]
    unnamed x2 -> x0, local copies, waits for them, and re-layouts: 4.13 us -> none
    pallas_call x0 -> x1, Pallas kernels: none -> 2.19 us  [per_device(): pl.pallas_call(place, out_shape=(jax.ShapeDtypeStruct(out.shape, BF16), j...]
where the time goes in v2:
time: 118 us
  Pallas kernels  117 us (99%)
    pallas_call x1, Pallas kernels, per_device(): pl.pallas_call(kernel, out_shape=(jax.ShapeDtypeStruct((512, 512), BF16),...  115 us

profile of v2, /device:TPU:1, one launch (start us, length us, event | category | flops | bytes accessed | tf_op | source)
XLA Modules:
  0.0 118.0 jit_solution(3325527912220823217)
XLA Ops:
  0.6 115.2 %grow.1 = (bf16[512,512]{1,0:T(8,128)(2,1)}, bf16[1024,512]{1,0:T(8,128)(2,1)}) custom-call(bf16[32,4096]{1,0:T(8,128)(2,1)} %sw.1, bf16[64,4096]{1,0:T(8,128)(2,1)} %eo.1, bf16[512,4096]{1,0:T(8,128)(2,1)} %ei_hbm.1, bf16[2,2,128,512]{3,2,1,0:T(8,128)(2,1)} %bitcast.2, bf16[2,2,128,512]{3,2,1,0:T(8,128)(2,1)} %bitcast.3), custom_call_target="tpu_custom_call" | custom-call | flops 9699999744 | bytes 8000000 | tf_op jit(solution)/shard_map/grow/pallas_call | solution.py:591
  115.8 2.2 %place.1 = (bf16[512,512]{1,0:T(8,128)(2,1)}, bf16[1024,512]{1,0:T(8,128)(2,1)}) custom-call(bf16[512,512]{1,0:T(8,128)(2,1)} %get-tuple-element.4.out_in, bf16[1024,512]{1,0:T(8,128)(2,1)} %get-tuple-element.5.grad_in), custom_call_target="tpu_custom_call" | custom-call | tf_op jit(solution)/shard_map/place/pallas_call | solution.py:649

commit v3 on v2

--- a/solution.py
+++ b/solution.py
@@ -1,3 +1,5 @@
+import math
+
 import jax
 import jax.numpy as jnp
 from jax import lax
@@ -8,7 +10,10 @@
 MESH = pl.DeviceIdType.MESH
 F32 = jnp.float32
 BF16 = jnp.bfloat16
-N_SEM = 160
+N_RECV, N_SEND, LONE = 92, 14, 8
+GROUP = 4 * 2**20
+PARTS = 4
+WIDE = 512 // PARTS
 
 
 def dot(a, b, dims):
@@ -103,28 +108,31 @@
     for i in range(4):
         expected += greet_unless_self(at(x=e_src_x, y=2 * k + i // 2, k=i % 2))
     count = [0]
-    sent = []
+    loads = [0]
+    lone = []
 
     def ids(n):
         first = count[0]
         count[0] += n
-        assert count[0] <= N_SEM
+        assert count[0] <= N_RECV
         return first
 
-    def remote(src, dst, to, s, r=None):
+    def remote(src, dst, to, s, r):
         return pltpu.make_async_remote_copy(
-            src_ref=src, dst_ref=dst, send_sem=ssem.at[s], recv_sem=rsem.at[s if r is None else r],
+            src_ref=src, dst_ref=dst, send_sem=ssem.at[s], recv_sem=rsem.at[r],
             device_id=to, device_id_type=MESH,
         )
 
-    def send(src, dst, to, s, r=None):
-        copy = remote(src, dst, to, s, r)
-        copy.start()
-        sent.append((copy, None))
-
-    def send_or_copy(src, dst, to, s, r):
+    def send(src, dst, to, r):
+        size = 2 * math.prod(src.shape)
+        if loads[-1] + size > GROUP:
+            loads.append(0)
+        loads[-1] += size
+        remote(src, dst, to, LONE + len(loads) - 1, r).start()
+
+    def send_or_copy(src, dst, to, r):
         mine = jnp.logical_and(to[0] == row, to[1] == col)
-        copy = remote(src, dst, to, s, r)
+        copy = remote(src, dst, to, len(lone), r)
 
         @pl.when(mine)
         def _():
@@ -134,15 +142,15 @@
         def _():
             copy.start()
 
-        sent.append((copy, jnp.logical_not(mine)))
+        lone.append((copy, jnp.logical_not(mine)))
 
     def arrived(ref, r):
-        remote(ref, ref, sib, r).wait_recv()
+        remote(ref, ref, sib, 0, r).wait_recv()
 
     class Gather:
         def __init__(self, slot, first, second, me, up, down):
             self.slot, self.first, self.second, self.me = slot, first, second, me
-            self.up, self.down, self.s = up, down, ids(4)
+            self.up, self.down, self.s = up, down, ids(3)
 
         def start(self):
             mine = self.slot(self.me)
@@ -157,17 +165,15 @@
         def pass_down(self):
             i = ring(self.me, 1)
             arrived(self.slot(i), self.s + 1)
-            send(self.second(i), self.second(i), self.down, self.s + 3)
+            send(self.second(i), self.second(i), self.down, self.s + 2)
 
         def finish(self):
-            i = ring(self.me, 2)
-            arrived(self.first(i), self.s + 2)
-            arrived(self.second(i), self.s + 3)
+            arrived(self.slot(ring(self.me, 2)), self.s + 2)
 
     class Scatter:
         def __init__(self, slot, first, second, tmp, two, me, up, down):
             self.slot, self.first, self.second = slot, first, second
-            self.tmp, self.two, self.me, self.up, self.down, self.s = tmp, two, me, up, down, ids(4)
+            self.tmp, self.two, self.me, self.up, self.down, self.s = tmp, two, me, up, down, ids(3)
 
         def start(self):
             i = ring(self.me, 2)
@@ -184,11 +190,10 @@
             i = ring(self.me, 3)
             arrived(self.tmp.at[1], self.s + 1)
             add_into(self.second(i), self.tmp.at[1])
-            send(self.slot(i), self.two.at[1], self.down, self.s + 3)
+            send(self.slot(i), self.two.at[1], self.down, self.s + 2)
 
         def finish(self):
-            arrived(self.two.at[0], self.s + 2)
-            arrived(self.two.at[1], self.s + 3)
+            arrived(self.two, self.s + 2)
 
     def add_into(dst, src):
         rows = dst.shape[0]
@@ -198,16 +203,15 @@
             part = pl.ds(pl.multiple_of(i * 64, 64), 64)
             dst[part] = (dst[part].astype(F32) + src[part].astype(F32)).astype(BF16)
 
-    sp, c1, a1, s1, e1, e2s, e2r = ids(2), ids(2), ids(1), ids(8), ids(4), ids(4), ids(4)
-    c2s, c2r = [ids(4), ids(4)], [ids(4), ids(4)]
+    sp, c1, a1, s1, e1, e2, c2 = ids(1), ids(2), ids(1), ids(1), ids(1), ids(1), ids(1)
     t1, t3, u1 = ids(4), ids(2), ids(2)
-    u2, u4 = [ids(4), ids(4)], [ids(5), ids(5)]
-    c4 = [ids(5), ids(5)]
+    u2, u4 = ids(2), ids(2)
+    c4 = ids(PARTS)
     s_home = s_all.at[zl, x, pl.ds(pl.multiple_of(zh * 64 + k * 32, 32), 32)]
 
     def spread_send():
         for n, to in enumerate((y_up, y_down)):
-            send(cot.at[:, 1, n * 64:n * 64 + 64], c_spread.at[:, n * 64:n * 64 + 64], to, sp + n)
+            send(cot.at[:, 1, n * 64:n * 64 + 64], c_spread.at[:, n * 64:n * 64 + 64], to, sp)
 
     def c1_send(half):
         src = cot.at[1 - zh, 0] if half == 0 else c_spread.at[1 - zh]
@@ -221,11 +225,7 @@
             src = c1_in.at[half]
         else:
             src = c_spread.at[zh] if half else cot.at[zh, 0]
-        for j in range(2):
-            send_or_copy(
-                src.at[:, j * 256:(j + 1) * 256], c_all.at[k, j, y, x], at(x=c_x[other][half]),
-                c2s[j] + 2 * other + half, c2r[j] + x,
-            )
+        send_or_copy(src, c_all.at[k, y, x], at(x=c_x[other][half]), c2)
 
     def s1_send():
         for dz in (1, 3, 2, 0):
@@ -233,7 +233,7 @@
                 tz, tk = ring(z, dz), (k + dk) % 2
                 piece = sw.at[:, pl.ds(pl.multiple_of(((tz // 2) * 2 + tk) * 1024, 1024), 1024)]
                 if dz or dk:
-                    send(piece, s_home, at(z=tz, k=tk), s1 + dz * 2 + dk)
+                    send(piece, s_home, at(z=tz, k=tk), s1)
                 else:
                     pltpu.make_async_copy(piece, s_home, rsem.at[s1]).start()
 
@@ -242,19 +242,17 @@
             i = ring(z, d)
             piece = eo.at[:, pl.ds(pl.multiple_of(i * 1024, 1024), 1024)]
             if d:
-                send(piece, e_z.at[z], at(z=i), e1 + d)
+                send(piece, e_z.at[z], at(z=i), e1)
             else:
                 pltpu.make_async_copy(piece, e_z.at[z], rsem.at[e1]).start()
 
     def e2_send():
-        for d in range(4):
-            arrived(e_z.at[ring(z, 4 - d)], e1 + d)
+        arrived(e_z, e1)
         for i in range(4):
-            send_or_copy(e_z.at[i], e_all.at[e_x[i], y0 * 2 + k], e_to[i], e2s + i, e2r + y0 * 2 + k)
+            send_or_copy(e_z.at[i], e_all.at[e_x[i], y0 * 2 + k], e_to[i], e2)
 
     def e_enter():
-        for i in range(4):
-            arrived(e_all.at[x, i], e2r + i)
+        arrived(e_all.at[x], e2)
         e_ring.start()
 
     s_ring = Gather(lambda i: s_all.at[:, i], lambda i: s_all.at[0, i], lambda i: s_all.at[1, i], x, x_up, x_down)
@@ -268,12 +266,15 @@
     e_ring = Gather(
         lambda i: e_all.at[i], lambda i: e_all.at[i, 0:2], lambda i: e_all.at[i, 2:4], x, x_up, x_down
     )
+    def c_block(kk, j, i, part=slice(None), toks=slice(None)):
+        return c_all.at[kk, i, part, toks, j * WIDE:(j + 1) * WIDE]
+
     c_ring = [
         Gather(
-            lambda i, j=j: c_all.at[k, j, i], lambda i, j=j: c_all.at[k, j, i, 0:2],
-            lambda i, j=j: c_all.at[k, j, i, 2:4], y, y_up, y_down,
-        )
-        for j in range(2)
+            lambda i, j=j: c_block(k, j, i), lambda i, j=j: c_block(k, j, i, slice(0, 2)),
+            lambda i, j=j: c_block(k, j, i, slice(2, 4)), y, y_up, y_down,
+        )
+        for j in range(PARTS)
     ]
     t_ring = [
         Gather(
@@ -301,10 +302,10 @@
     )
     g_sum = [
         Scatter(
-            lambda i, j=j: g_part.at[j, i], lambda i, j=j: g_part.at[j, i, 0:256],
-            lambda i, j=j: g_part.at[j, i, 256:512], g_tmp.at[j], g_two.at[j], z, z_up, z_down,
-        )
-        for j in range(2)
+            lambda i, j=j: g_part.at[j, i], lambda i, j=j: g_part.at[j, i, 0:WIDE],
+            lambda i, j=j: g_part.at[j, i, WIDE:2 * WIDE], g_tmp.at[j], g_two.at[j], z, z_up, z_down,
+        )
+        for j in range(PARTS)
     ]
     o_sum = [
         Scatter(
@@ -346,46 +347,37 @@
         t_dots(d, k, t_own)
     for d in order[1:]:
         t_join(d)
-    for n in range(2):
-        arrived(c_spread.at[:, n * 64:n * 64 + 64], sp + n)
+    arrived(c_spread, sp)
     c1_send(1)
     c2_send(0, 1)
     arrived(c1_in.at[0], c1)
     c2_send(1, 0)
-    s1_send()
     t_sum.pass_up()
     t_sum.pass_down()
+    arrived(c1_in.at[1], c1 + 1)
+    c2_send(1, 1)
+    s1_send()
+    e1_send()
 
     def c_enter(j):
-        for i in range(4):
-            arrived(c_all.at[k, j, y, i], c2r[j] + i)
+        if j == 0:
+            arrived(c_all.at[k, y], c2)
         c_ring[j].start()
-        send(c_all.at[k, j, y], c_all.at[k, j, y], sib, c4[j])
+        send(c_block(k, j, y), c_block(k, j, y), sib, c4 + j)
 
     def c_pass(j):
         c_ring[j].pass_up()
         c_ring[j].pass_down()
-        for n, d in ((1, 3), (2, 1)):
-            send(c_all.at[k, j, ring(y, d)], c_all.at[k, j, ring(y, d)], sib, c4[j] + n)
+        for d in (3, 1):
+            send(c_block(k, j, ring(y, d)), c_block(k, j, ring(y, d)), sib, c4 + j)
 
     def c_finish(j):
         c_ring[j].finish()
-        for n, half in ((3, slice(0, 2)), (4, slice(2, 4))):
-            send(c_all.at[k, j, ring(y, 2), half], c_all.at[k, j, ring(y, 2), half], sib, c4[j] + n)
+        for half in (slice(0, 2), slice(2, 4)):
+            send(c_block(k, j, ring(y, 2), half), c_block(k, j, ring(y, 2), half), sib, c4 + j)
 
     def c_sibling(j):
-        for n, d in ((0, 0), (1, 3), (2, 1)):
-            arrived(c_all.at[1 - k, j, ring(y, d)], c4[j] + n)
-        for n, half in ((3, slice(0, 2)), (4, slice(2, 4))):
-            arrived(c_all.at[1 - k, j, ring(y, 2), half], c4[j] + n)
-
-    arrived(a_all.at[:, x, :, a_cols(1 - zh)], a1)
-    a_ring[1].start()
-    arrived(c1_in.at[1], c1 + 1)
-    c2_send(1, 1)
-    a_ring[0].pass_up()
-    a_ring[0].pass_down()
-    c_enter(0)
+        arrived(c_all.at[1 - k, :, :, :, j * WIDE:(j + 1) * WIDE], c4 + j)
 
     def t_enter(c):
         rows = slice(c * 256, c * 256 + 256)
@@ -393,65 +385,87 @@
         t_all[y, rows] = (t_own[0, zh, rows] + t_swap_in[rows].astype(F32)).astype(BF16)
         t_ring[c].start()
 
-    t_sum.finish()
-    for c in range(2):
-        rows = slice(c * 256, c * 256 + 256)
+    def g_block(j):
+        parts = (
+            (0, slice(None), a_all.at[0]),
+            (1, slice(0, 64), a_all.at[1, :, 0:64]),
+            (3, slice(64, 128), a_all.at[1, :, 64:128]),
+        )
         for half in range(2):
-            t_own[0, half, rows] = (
-                t_part[y, half, rows].astype(F32)
-                + t_two[0, half, rows].astype(F32)
-                + t_two[1, half, rows].astype(F32)
-            )
-        t_swap[rows] = t_own[0, 1 - zh, rows].astype(BF16)
-        send(t_swap.at[rows], t_swap_in.at[rows], z_far, t3 + c)
-    e1_send()
-    a_ring[1].pass_up()
-    a_ring[1].pass_down()
-    for i in range(8):
-        arrived(s_home, s1 + i)
-    s_ring.start()
+            total = None
+            for d, toks, acts in parts:
+                block = jnp.concatenate(
+                    [
+                        c_block(kk, j, ring(2 * v + x1, d), toks=toks)[...].reshape(-1, WIDE)
+                        for v in range(2)
+                        for kk in range(2)
+                    ],
+                    axis=1,
+                )
+                part = dot(block, acts[:, :, half * 512:half * 512 + 512].reshape(-1, 512), ((0,), (0,)))
+                total = part if total is None else total + part
+            total = total.astype(BF16)
+            for v in range(2):
+                g_part[j, half * 2 + v] = total[v * 2 * WIDE:(v + 1) * 2 * WIDE]
+
+    def g_enter(j):
+        c_sibling(j)
+        g_block(j)
+        g_sum[j].start()
+
+    def g_pass(j):
+        g_sum[j].pass_up()
+        g_sum[j].pass_down()
+
+    def t_leave():
+        t_sum.finish()
+        for c in range(2):
+            rows = slice(c * 256, c * 256 + 256)
+            for half in range(2):
+                t_own[0, half, rows] = (
+                    t_part[y, half, rows].astype(F32)
+                    + t_two[0, half, rows].astype(F32)
+                    + t_two[1, half, rows].astype(F32)
+                )
+            t_swap[rows] = t_own[0, 1 - zh, rows].astype(BF16)
+            send(t_swap.at[rows], t_swap_in.at[rows], z_far, t3 + c)
+
+    def t_pass():
+        for c in range(2):
+            t_ring[c].pass_up()
+            t_ring[c].pass_down()
+
+    def both(gather):
+        gather.pass_up()
+        gather.pass_down()
+
+    arrived(a_all.at[:, x, :, a_cols(1 - zh)], a1)
+    a_ring[1].start()
+    both(a_ring[0])
+    c_enter(0)
+    both(a_ring[1])
+    t_leave()
     c_pass(0)
     c_enter(1)
-    t_enter(0)
-    t_enter(1)
+    c_enter(2)
+    arrived(s_all.at[:, x], s1)
+    s_ring.start()
     c_finish(0)
     for ring_of_a in a_ring:
         ring_of_a.finish()
-    c_sibling(0)
-
-    def g_block(j):
-        @pl.loop(0, 4)
-        def _(n):
-            v, kk = n // 2, n % 2
-            home = 2 * v + x1
-            for half in range(2):
-                cols = slice(half * 512, half * 512 + 512)
-                total = dot(
-                    c_all[kk, j, home].reshape(512, 256), a_all[0, :, :, cols].reshape(512, 512), ((0,), (0,))
-                )
-                for d, toks in ((1, slice(0, 64)), (3, slice(64, 128))):
-                    total += dot(
-                        c_all[kk, j, ring(home, d), :, toks].reshape(256, 256),
-                        a_all[1, :, toks, cols].reshape(256, 512), ((0,), (0,)),
-                    )
-                g_part[j, half * 2 + v, pl.ds(pl.multiple_of(kk * 256, 256), 256)] = total.astype(BF16)
-
-    g_block(0)
-    g_sum[0].start()
-    t_ring[0].pass_up()
-    t_ring[0].pass_down()
+    g_enter(0)
     c_pass(1)
-    t_ring[1].pass_up()
-    t_ring[1].pass_down()
-    s_ring.pass_up()
-    s_ring.pass_down()
-    g_sum[0].pass_up()
-    g_sum[0].pass_down()
+    t_enter(0)
+    t_enter(1)
+    c_pass(2)
+    g_pass(0)
+    c_finish(1)
+    g_enter(1)
+    t_pass()
+    c_enter(3)
+    both(s_ring)
     e2_send()
-    c_finish(1)
-    c_sibling(1)
-    g_block(1)
-    g_sum[1].start()
+    g_pass(1)
 
     def u_dot(c, n):
         total = None
@@ -474,42 +488,42 @@
         arrived(u_sib_in.at[c], u1 + c)
         u_part[c] = (u_own[c, k] + u_sib_in[c].astype(F32)).astype(BF16)
         for d in (1, 3, 2):
-            send(u_part.at[c, ring(z, d)], u_in.at[c, d], at(z=ring(z, d)), u2[c] + d)
+            send(u_part.at[c, ring(z, d)], u_in.at[c, d], at(z=ring(z, d)), u2 + c)
     e_enter()
+    c_finish(2)
+    g_enter(2)
+    c_pass(3)
 
     def u_enter(c):
         rows = slice(c * 256, c * 256 + 256)
-        for d in (1, 3, 2):
-            arrived(u_in.at[c, d], u2[c] + d)
+        arrived(u_in.at[c, 1:4], u2 + c)
         u_all[zl, rows, u_cols(k, y)] = (u_part[c, z].astype(F32) + u_in[c, 2].astype(F32)).astype(BF16)
         u_all[1 - zl, rows, u_cols(k, y)] = (u_in[c, 1].astype(F32) + u_in[c, 3].astype(F32)).astype(BF16)
         u_ring[c].start()
-        send(u_block(c, k, y), u_block(c, k, y), sib, u4[c])
+        send(u_block(c, k, y), u_block(c, k, y), sib, u4 + c)
 
     def u_pass(c):
         u_ring[c].pass_up()
         u_ring[c].pass_down()
-        for n, d in ((1, 3), (2, 1)):
-            send(u_block(c, k, ring(y, d)), u_block(c, k, ring(y, d)), sib, u4[c] + n)
+        for d in (3, 1):
+            send(u_block(c, k, ring(y, d)), u_block(c, k, ring(y, d)), sib, u4 + c)
 
     def u_finish(c):
         u_ring[c].finish()
         for n in range(2):
             half = u_block(c, k, ring(y, 2), n)
-            send(half, half, sib, u4[c] + 3 + n)
-        for n, d in ((0, 0), (1, 3), (2, 1)):
-            arrived(u_block(c, 1 - k, ring(y, d)), u4[c] + n)
-        for n in range(2):
-            arrived(u_block(c, 1 - k, ring(y, 2), n), u4[c] + 3 + n)
+            send(half, half, sib, u4 + c)
+        arrived(u_all.at[:, c * 256:c * 256 + 256, pl.ds(pl.multiple_of((1 - k) * 512, 512), 512)], u4 + c)
 
     u_enter(0)
     u_enter(1)
-    g_sum[1].pass_up()
-    g_sum[1].pass_down()
-    e_ring.pass_up()
-    e_ring.pass_down()
+    g_pass(2)
+    c_finish(3)
+    g_enter(3)
+    both(e_ring)
     u_pass(0)
     u_pass(1)
+    g_pass(3)
     u_finish(0)
     e_ring.finish()
 
@@ -532,37 +546,37 @@
     u_finish(1)
     o_block(1)
     o_sum[1].start()
-    g_sum[0].finish()
     o_sum[0].pass_up()
     o_sum[0].pass_down()
     o_sum[1].pass_up()
     o_sum[1].pass_down()
 
-    def last(dst, part, two, first, to):
-        @pl.loop(0, 4)
+    def last(dst, part, two, rows, first, to):
+        @pl.loop(0, rows // 64)
         def _(i):
             src = pl.ds(pl.multiple_of(first + i * 64, 64), 64)
             dst[pl.ds(pl.multiple_of(to + i * 64, 64), 64)] = (
                 part[src].astype(F32) + two[0, src].astype(F32) + two[1, src].astype(F32)
             ).astype(BF16)
 
-    g_sum[1].finish()
-    for j in range(2):
+    for j in range(PARTS):
+        g_sum[j].finish()
         for kk in range(2):
-            last(grad_v, g_part.at[j, z], g_two.at[j], kk * 256, kk * 512 + j * 256)
+            last(grad_v, g_part.at[j, z], g_two.at[j], WIDE, kk * WIDE, kk * 512 + j * WIDE)
     writes = [pltpu.make_async_copy(grad_v, grad_ref, out_sem.at[0])]
     writes[0].start()
     for c in range(2):
         o_sum[c].finish()
         rows = slice(c * 256, c * 256 + 256)
-        last(out_v, o_part.at[c, z], o_two.at[c], 0, c * 256)
+        last(out_v, o_part.at[c, z], o_two.at[c], 256, 0, c * 256)
         writes.append(pltpu.make_async_copy(out_v.at[rows], out_ref.at[rows], out_sem.at[1 + c]))
         writes[-1].start()
-    for copy, when in sent:
-        if when is None:
-            copy.wait_send()
-        else:
-            pl.when(when)(copy.wait_send)
+    assert len(lone) <= LONE and len(loads) <= N_SEND - LONE
+    for copy, when in lone:
+        pl.when(when)(copy.wait_send)
+    for n, size in enumerate(loads):
+        rows = ei_hbm.at[0:size // 8192]
+        remote(rows, rows, sib, LONE + n, 0).wait_send()
     for copy in writes:
         copy.wait()
 
@@ -607,7 +621,7 @@
             buf(1024, 512),
             pltpu.SemaphoreType.DMA((3,)),
             buf(2, 4, 128, 1024),
-            buf(2, 2, 4, 4, 128, 256),
+            buf(2, 4, 4, 128, 512),
             buf(2, 128, 512),
             buf(2, 128, 512),
             buf(4, 2, 512, 256),
@@ -628,11 +642,11 @@
             buf(2, 4, 256, 512),
             buf(2, 2, 128, 512),
             buf(2, 2, 256, 512),
-            buf(2, 4, 512, 512),
-            buf(2, 2, 256, 512),
-            buf(2, 2, 512, 512),
-            pltpu.SemaphoreType.DMA((N_SEM,)),
-            pltpu.SemaphoreType.DMA((N_SEM,)),
+            buf(PARTS, 4, 2 * WIDE, 512),
+            buf(PARTS, 2, WIDE, 512),
+            buf(PARTS, 2, 2 * WIDE, 512),
+            pltpu.SemaphoreType.DMA((N_SEND,)),
+            pltpu.SemaphoreType.DMA((N_RECV,)),
         ],
         compiler_params=pltpu.CompilerParams(
             collective_id=0, has_side_effects=True, vmem_limit_bytes=58 * 2**20

time: 118 us -> 114 us (0.966)
  Pallas kernels: 117 us -> 113 us
    pallas_call x1, Pallas kernels: 115 us -> 111 us  [per_device(): pl.pallas_call(kernel, out_shape=(jax.ShapeDtypeStruct((512, 512), BF16),...]
where the time goes in v3:
time: 114 us
  Pallas kernels  113 us (99%)
    pallas_call x1, Pallas kernels, per_device(): pl.pallas_call(kernel, out_shape=(jax.ShapeDtypeStruct((512, 512), BF16),...  111 us

profile of v3, /device:TPU:1, one launch (start us, length us, event | category | flops | bytes accessed | tf_op | source)
XLA Modules:
  0.0 113.6 jit_solution(17092344340039415899)
XLA Ops:
  0.6 110.6 %grow.1 = (bf16[512,512]{1,0:T(8,128)(2,1)}, bf16[1024,512]{1,0:T(8,128)(2,1)}) custom-call(bf16[32,4096]{1,0:T(8,128)(2,1)} %sw.1, bf16[64,4096]{1,0:T(8,128)(2,1)} %eo.1, bf16[512,4096]{1,0:T(8,128)(2,1)} %ei_hbm.1, bf16[2,2,128,512]{3,2,1,0:T(8,128)(2,1)} %bitcast.2, bf16[2,2,128,512]{3,2,1,0:T(8,128)(2,1)} %bitcast.3), custom_call_target="tpu_custom_call" | custom-call | flops 9699999744 | bytes 8000000 | tf_op jit(solution)/shard_map/grow/pallas_call | solution.py:605
  111.2 2.2 %place.1 = (bf16[512,512]{1,0:T(8,128)(2,1)}, bf16[1024,512]{1,0:T(8,128)(2,1)}) custom-call(bf16[512,512]{1,0:T(8,128)(2,1)} %get-tuple-element.4.out_in, bf16[1024,512]{1,0:T(8,128)(2,1)} %get-tuple-element.5.grad_in), custom_call_target="tpu_custom_call" | custom-call | tf_op jit(solution)/shard_map/place/pallas_call | solution.py:663

commit v4 on v3

--- a/solution.py
+++ b/solution.py
@@ -10,7 +10,7 @@
 MESH = pl.DeviceIdType.MESH
 F32 = jnp.float32
 BF16 = jnp.bfloat16
-N_RECV, N_SEND, LONE = 92, 14, 8
+N_RECV, N_SEND, LONE = 96, 18, 12
 GROUP = 4 * 2**20
 PARTS = 4
 WIDE = 512 // PARTS
@@ -22,7 +22,7 @@
 
 def kernel(
     sw, eo, ei_hbm, act_hbm, cot, out_ref, grad_ref,
-    ei, act, in_sem, s_all, e_z, e_all, out_v, grad_v, out_sem, a_all, c_all, c_spread, c1_in,
+    ei, act, in_sem, s_all, e_z, e_all,  a_all, c_all, c_spread, c1_in,
     t_sib, t_sib_in, t_own, t_part, t_tmp, t_two, t_swap, t_swap_in, t_all,
     u_own, u_sib, u_sib_in, u_part, u_in, u_all,
     o_part, o_tmp, o_two, g_part, g_tmp, g_two,
@@ -203,7 +203,7 @@
             part = pl.ds(pl.multiple_of(i * 64, 64), 64)
             dst[part] = (dst[part].astype(F32) + src[part].astype(F32)).astype(BF16)
 
-    sp, c1, a1, s1, e1, e2, c2 = ids(1), ids(2), ids(1), ids(1), ids(1), ids(1), ids(1)
+    sp, c1, a1, s1, e1, e2, c2 = ids(1), ids(2), ids(1), ids(1), ids(1), ids(2), ids(1)
     t1, t3, u1 = ids(4), ids(2), ids(2)
     u2, u4 = ids(2), ids(2)
     c4 = ids(PARTS)
@@ -246,14 +246,18 @@
             else:
                 pltpu.make_async_copy(piece, e_z.at[z], rsem.at[e1]).start()
 
+    def e_cols(h):
+        return slice(h * 512, h * 512 + 512)
+
     def e2_send():
         arrived(e_z, e1)
-        for i in range(4):
-            send_or_copy(e_z.at[i], e_all.at[e_x[i], y0 * 2 + k], e_to[i], e2)
-
-    def e_enter():
-        arrived(e_all.at[x], e2)
-        e_ring.start()
+        for h in range(2):
+            for i in range(4):
+                send_or_copy(e_z.at[i, :, e_cols(h)], e_all.at[e_x[i], y0 * 2 + k, :, e_cols(h)], e_to[i], e2 + h)
+
+    def e_enter(h):
+        arrived(e_all.at[x, :, :, e_cols(h)], e2 + h)
+        e_ring[h].start()
 
     s_ring = Gather(lambda i: s_all.at[:, i], lambda i: s_all.at[0, i], lambda i: s_all.at[1, i], x, x_up, x_down)
     a_ring = [
@@ -263,9 +267,14 @@
         )
         for c in (a_cols(zh), a_cols(1 - zh))
     ]
-    e_ring = Gather(
-        lambda i: e_all.at[i], lambda i: e_all.at[i, 0:2], lambda i: e_all.at[i, 2:4], x, x_up, x_down
-    )
+    e_ring = [
+        Gather(
+            lambda i, h=h: e_all.at[i, :, :, e_cols(h)], lambda i, h=h: e_all.at[i, 0:2, :, e_cols(h)],
+            lambda i, h=h: e_all.at[i, 2:4, :, e_cols(h)], x, x_up, x_down,
+        )
+        for h in range(2)
+    ]
+
     def c_block(kk, j, i, part=slice(None), toks=slice(None)):
         return c_all.at[kk, i, part, toks, j * WIDE:(j + 1) * WIDE]
 
@@ -324,11 +333,14 @@
         for half in range(2):
             t_part[ring(y, d), half] = (t_own[d, half] + t_sib_in[d, half].astype(F32)).astype(BF16)
 
-    act_copy.wait()
-    for d in order:
+    def ei_wait(d):
         for copy in ei_copies(d):
             copy.wait()
+
+    act_copy.wait()
+    ei_wait(2)
     t_dots(2, 1 - k, t_sib)
+    t_dots(2, k, t_own)
     a_own_copy.wait()
     pl.semaphore_wait(barrier, expected)
     send(t_sib.at[2], t_sib_in.at[2], sib, t1 + 2)
@@ -336,9 +348,8 @@
     c1_send(0)
     c2_send(0, 0)
     a_ring[0].start()
-    a1_send()
-    t_dots(2, k, t_own)
     for d in order[1:]:
+        ei_wait(d)
         t_dots(d, 1 - k, t_sib)
         send(t_sib.at[d], t_sib_in.at[d], sib, t1 + d)
     t_join(2)
@@ -349,6 +360,7 @@
         t_join(d)
     arrived(c_spread, sp)
     c1_send(1)
+    a1_send()
     c2_send(0, 1)
     arrived(c1_in.at[0], c1)
     c2_send(1, 0)
@@ -356,8 +368,8 @@
     t_sum.pass_down()
     arrived(c1_in.at[1], c1 + 1)
     c2_send(1, 1)
+    e1_send()
     s1_send()
-    e1_send()
 
     def c_enter(j):
         if j == 0:
@@ -458,13 +470,15 @@
     t_enter(0)
     t_enter(1)
     c_pass(2)
+    c_finish(1)
     g_pass(0)
-    c_finish(1)
     g_enter(1)
     t_pass()
-    c_enter(3)
     both(s_ring)
     e2_send()
+    c_enter(3)
+    c_finish(2)
+    g_enter(2)
     g_pass(1)
 
     def u_dot(c, n):
@@ -484,15 +498,17 @@
             u_own[c, n % 2, n // 2] = u_dot(c, n)
         u_sib[c] = u_own[c, 1 - k].astype(BF16)
         send(u_sib.at[c], u_sib_in.at[c], sib, u1 + c)
+    e_enter(0)
+    c_pass(3)
     for c in range(2):
         arrived(u_sib_in.at[c], u1 + c)
         u_part[c] = (u_own[c, k] + u_sib_in[c].astype(F32)).astype(BF16)
         for d in (1, 3, 2):
             send(u_part.at[c, ring(z, d)], u_in.at[c, d], at(z=ring(z, d)), u2 + c)
-    e_enter()
-    c_finish(2)
-    g_enter(2)
-    c_pass(3)
+    g_pass(2)
+    e_enter(1)
+    c_finish(3)
+    g_enter(3)
 
     def u_enter(c):
         rows = slice(c * 256, c * 256 + 256)
@@ -516,16 +532,15 @@
         arrived(u_all.at[:, c * 256:c * 256 + 256, pl.ds(pl.multiple_of((1 - k) * 512, 512), 512)], u4 + c)
 
     u_enter(0)
+    both(e_ring[0])
     u_enter(1)
-    g_pass(2)
-    c_finish(3)
-    g_enter(3)
-    both(e_ring)
     u_pass(0)
+    both(e_ring[1])
     u_pass(1)
     g_pass(3)
     u_finish(0)
-    e_ring.finish()
+    for ring_of_e in e_ring:
+        ring_of_e.finish()
 
     def o_block(c):
         for v in range(2):
@@ -562,54 +577,34 @@
     for j in range(PARTS):
         g_sum[j].finish()
         for kk in range(2):
-            last(grad_v, g_part.at[j, z], g_two.at[j], WIDE, kk * WIDE, kk * 512 + j * WIDE)
-    writes = [pltpu.make_async_copy(grad_v, grad_ref, out_sem.at[0])]
-    writes[0].start()
+            last(grad_ref, g_part.at[j, z], g_two.at[j], WIDE, kk * WIDE, kk * 512 + j * WIDE)
     for c in range(2):
         o_sum[c].finish()
         rows = slice(c * 256, c * 256 + 256)
-        last(out_v, o_part.at[c, z], o_two.at[c], 256, 0, c * 256)
-        writes.append(pltpu.make_async_copy(out_v.at[rows], out_ref.at[rows], out_sem.at[1 + c]))
-        writes[-1].start()
+        last(out_ref, o_part.at[c, z], o_two.at[c], 256, 0, c * 256)
     assert len(lone) <= LONE and len(loads) <= N_SEND - LONE
     for copy, when in lone:
         pl.when(when)(copy.wait_send)
     for n, size in enumerate(loads):
         rows = ei_hbm.at[0:size // 8192]
         remote(rows, rows, sib, LONE + n, 0).wait_send()
-    for copy in writes:
-        copy.wait()
-
-
-def place(out_in, grad_in, out_ref, grad_ref, rows, in_sem, out_sem):
-    parts = [(out_in, out_ref, i) for i in range(2)] + [(grad_in, grad_ref, i) for i in range(4)]
-    reads, writes = [], []
-    for n, (src, dst, i) in enumerate(parts):
-        part = pl.ds(i * 256, 256)
-        reads.append(pltpu.make_async_copy(src.at[part], rows.at[n], in_sem.at[n]))
-        writes.append(pltpu.make_async_copy(rows.at[n], dst.at[part], out_sem.at[n]))
-        reads[n].start()
-    for read, write in zip(reads, writes):
-        read.wait()
-        write.start()
-    for write in writes:
-        write.wait()
 
 
 def per_device(small_weight, expand_out, expand_in, activations, cotangent):
     hbm = pl.BlockSpec(memory_space=pl.ANY)
+    vmem = pl.BlockSpec(memory_space=pltpu.VMEM)
 
     def buf(*shape, dtype=BF16):
         return pltpu.VMEM(shape, dtype)
 
-    out, grad = pl.pallas_call(
+    return pl.pallas_call(
         kernel,
         out_shape=(
-            jax.ShapeDtypeStruct((512, 512), BF16),
-            jax.ShapeDtypeStruct((1024, 512), BF16),
+            pltpu.VMEM((512, 512), BF16),
+            pltpu.VMEM((1024, 512), BF16),
         ),
         in_specs=[hbm] * 5,
-        out_specs=(hbm, hbm),
+        out_specs=(vmem, vmem),
         scratch_shapes=[
             buf(4, 4, 512, 256),
             buf(2, 2, 128, 512),
@@ -617,9 +612,6 @@
             buf(2, 4, 128, 1024),
             buf(4, 64, 1024),
             buf(4, 4, 64, 1024),
-            buf(512, 512),
-            buf(1024, 512),
-            pltpu.SemaphoreType.DMA((3,)),
             buf(2, 4, 128, 1024),
             buf(2, 4, 4, 128, 512),
             buf(2, 128, 512),
@@ -660,15 +652,6 @@
         activations.reshape(2, 2, 128, 512),
         cotangent.reshape(2, 2, 128, 512),
     )
-    return pl.pallas_call(
-        place,
-        out_shape=(jax.ShapeDtypeStruct(out.shape, BF16), jax.ShapeDtypeStruct(grad.shape, BF16)),
-        in_specs=[hbm] * 2,
-        out_specs=(hbm, hbm),
-        scratch_shapes=[buf(6, 256, 512), pltpu.SemaphoreType.DMA((6,)), pltpu.SemaphoreType.DMA((6,))],
-        name="place",
-    )(out, grad)
-
 
 def solution(mesh):
     in_specs = (

time: 114 us -> 108 us (0.947)
  Pallas kernels: 113 us -> 106 us
  local copies, waits for them, and re-layouts: 0 us -> 1.77 us
    pallas_call x2 -> x1, Pallas kernels: 113 us -> 106 us  [per_device(): pl.pallas_call(kernel, out_shape=(pltpu.VMEM((512, 512), BF16), pltpu.VME...]
    unnamed x0 -> x2, local copies, waits for them, and re-layouts: none -> 1.77 us
where the time goes in v4:
time: 108 us
  Pallas kernels  106 us (98%)
  local copies, waits for them, and re-layouts  1.77 us (2%)
    pallas_call x1, Pallas kernels, per_device(): pl.pallas_call(kernel, out_shape=(pltpu.VMEM((512, 512), BF16), pltpu.VME...  106 us

profile of v4, /device:TPU:1, one launch (start us, length us, event | category | flops | bytes accessed | tf_op | source)
XLA Modules:
  0.0 107.9 jit_solution(2052893926218590823)
XLA Ops:
  0.6 105.5 %grow.1 = (bf16[512,512]{1,0:T(8,128)(2,1)S(1)}, bf16[1024,512]{1,0:T(8,128)(2,1)S(1)}) custom-call(bf16[32,4096]{1,0:T(8,128)(2,1)} %sw.1, bf16[64,4096]{1,0:T(8,128)(2,1)} %eo.1, bf16[512,4096]{1,0:T(8,128)(2,1)} %ei_hbm.1, bf16[2,2,128,512]{3,2,1,0:T(8,128)(2,1)} %bitcast.2, bf16[2,2,128,512]{3,2,1,0:T(8,128)(2,1)} %bitcast.3), custom_call_target="tpu_custom_call" | custom-call | flops 9699999744 | bytes 8000000 | tf_op jit(solution)/shard_map/grow/pallas_call | solution.py:600
  106.2 0.8 copy.9
  106.9 1.0 copy.10

commit v5 on v4

--- a/solution.py
+++ b/solution.py
@@ -344,8 +344,8 @@
     a_own_copy.wait()
     pl.semaphore_wait(barrier, expected)
     send(t_sib.at[2], t_sib_in.at[2], sib, t1 + 2)
+    c1_send(0)
     spread_send()
-    c1_send(0)
     c2_send(0, 0)
     a_ring[0].start()
     for d in order[1:]:
@@ -503,7 +503,7 @@
     for c in range(2):
         arrived(u_sib_in.at[c], u1 + c)
         u_part[c] = (u_own[c, k] + u_sib_in[c].astype(F32)).astype(BF16)
-        for d in (1, 3, 2):
+        for d in (2, 1, 3):
             send(u_part.at[c, ring(z, d)], u_in.at[c, d], at(z=ring(z, d)), u2 + c)
     g_pass(2)
     e_enter(1)
@@ -542,25 +542,25 @@
     for ring_of_e in e_ring:
         ring_of_e.finish()
 
-    def o_block(c):
-        for v in range(2):
-            for w in range(2):
-                slot = 2 * y0 + v
-                if w:
-                    slot = outer(slot)
-                weight = e_all[slot].reshape(256, 1024)
-                for tok in range(2):
-                    total = dot(u_all[tok, c * 256:c * 256 + 256], weight, ((1,), (1,))).astype(BF16)
-                    for n in range(2):
-                        o_part[c, v * 2 + tok, :, n * 256 + w * 128:n * 256 + w * 128 + 128] = total[
-                            :, n * 128:n * 128 + 128
-                        ]
-
-    o_block(0)
-    o_sum[0].start()
+    def o_shard(c, v, tok):
+        for w in range(2):
+            slot = 2 * y0 + v
+            if w:
+                slot = outer(slot)
+            weight = e_all[slot].reshape(256, 1024)
+            total = dot(u_all[tok, c * 256:c * 256 + 256], weight, ((1,), (1,))).astype(BF16)
+            for n in range(2):
+                o_part[c, v * 2 + tok, :, n * 256 + w * 128:n * 256 + w * 128 + 128] = total[:, n * 128:n * 128 + 128]
+
+    def o_enter(c):
+        o_shard(c, 1 - zh, zl)
+        o_sum[c].start()
+        for v, tok in ((zh, 1 - zl), (1 - zh, 1 - zl), (zh, zl)):
+            o_shard(c, v, tok)
+
+    o_enter(0)
     u_finish(1)
-    o_block(1)
-    o_sum[1].start()
+    o_enter(1)
     o_sum[0].pass_up()
     o_sum[0].pass_down()
     o_sum[1].pass_up()

time: 108 us -> 108 us (level)
  no operation moved by 1% of the time
where the time goes in v5:
time: 108 us; the launch traced here: 107 us
  Pallas kernels  105 us (97%)
  local copies, waits for them, and re-layouts  1.77 us (2%)
    pallas_call x1, Pallas kernels, per_device(): pl.pallas_call(kernel, out_shape=(pltpu.VMEM((512, 512), BF16), pltpu.VME...  105 us

profile of v5, /device:TPU:1, one launch (start us, length us, event | category | flops | bytes accessed | tf_op | source)
XLA Modules:
  0.0 107.5 jit_solution(7135852649751894036)
XLA Ops:
  0.6 105.1 %grow.1 = (bf16[512,512]{1,0:T(8,128)(2,1)S(1)}, bf16[1024,512]{1,0:T(8,128)(2,1)S(1)}) custom-call(bf16[32,4096]{1,0:T(8,128)(2,1)} %sw.1, bf16[64,4096]{1,0:T(8,128)(2,1)} %eo.1, bf16[512,4096]{1,0:T(8,128)(2,1)} %ei_hbm.1, bf16[2,2,128,512]{3,2,1,0:T(8,128)(2,1)} %bitcast.2, bf16[2,2,128,512]{3,2,1,0:T(8,128)(2,1)} %bitcast.3), custom_call_target="tpu_custom_call" | custom-call | flops 9699999744 | bytes 8000000 | tf_op jit(solution)/shard_map/grow/pallas_call | solution.py:600
  105.7 0.8 copy.9
  106.5 1.0 copy.10

commit v6 on v5

--- a/solution.py
+++ b/solution.py
@@ -364,12 +364,12 @@
     c2_send(0, 1)
     arrived(c1_in.at[0], c1)
     c2_send(1, 0)
+    s1_send()
     t_sum.pass_up()
     t_sum.pass_down()
     arrived(c1_in.at[1], c1 + 1)
     c2_send(1, 1)
     e1_send()
-    s1_send()
 
     def c_enter(j):
         if j == 0:

time: 108 us -> 108 us (level)
  no operation moved by 1% of the time
where the time goes in v6:
time: 108 us; the launch traced here: 107 us
  Pallas kernels  105 us (97%)
  local copies, waits for them, and re-layouts  1.77 us (2%)
    pallas_call x1, Pallas kernels, per_device(): pl.pallas_call(kernel, out_shape=(pltpu.VMEM((512, 512), BF16), pltpu.VME...  105 us

profile of v6, /device:TPU:1, one launch (start us, length us, event | category | flops | bytes accessed | tf_op | source)
XLA Modules:
  0.0 107.5 jit_solution(3559343022890258566)
XLA Ops:
  0.6 105.1 %grow.1 = (bf16[512,512]{1,0:T(8,128)(2,1)S(1)}, bf16[1024,512]{1,0:T(8,128)(2,1)S(1)}) custom-call(bf16[32,4096]{1,0:T(8,128)(2,1)} %sw.1, bf16[64,4096]{1,0:T(8,128)(2,1)} %eo.1, bf16[512,4096]{1,0:T(8,128)(2,1)} %ei_hbm.1, bf16[2,2,128,512]{3,2,1,0:T(8,128)(2,1)} %bitcast.2, bf16[2,2,128,512]{3,2,1,0:T(8,128)(2,1)} %bitcast.3), custom_call_target="tpu_custom_call" | custom-call | flops 9699999744 | bytes 8000000 | tf_op jit(solution)/shard_map/grow/pallas_call | solution.py:600
  105.7 0.8 copy.9
  106.5 1.0 copy.10
